TPU v7x, 32 devices: a whole 2x2x4 slice. The times are simulated.
32 devices in a mesh: dp: 16 (over z, y, core), fsdp: 2 (over x).
Axes of the slice: x: 2, y: 2, z: 4, core: 2. Of those that a mesh axis runs over, the one named last changes fastest.
Arguments:
- tokens: bfloat16 [24576, 1024], P(('dp', 'fsdp')), may hold values from -6 to 6
- lengths: int32 [64, 3], P(('dp', 'fsdp')), may hold values from 1 to 288, 384 in all within a row
- cotangent: bfloat16 [24576, 1024], P(('dp', 'fsdp')), may hold values from -6 to 6
- qkv_weight: bfloat16 [1024, 3072], P(('dp', 'fsdp')), may hold values from -0.1875 to 0.1875
- query_value_bias: bfloat16 [2048], P(('dp', 'fsdp')), may hold values from -1.5 to 1.5
- dense_weight: bfloat16 [1024, 1024], P(('dp', 'fsdp')), may hold values from -0.5 to 0.5
- dense_bias: bfloat16 [1024], P(('dp', 'fsdp')), may hold values from -1.5 to 1.5
- up_weight: bfloat16 [1024, 4096], P(('dp', 'fsdp')), may hold values from -0.1875 to 0.1875
- up_bias: bfloat16 [4096], P(('dp', 'fsdp')), may hold values from -2.5 to 2.5
- down_weight: bfloat16 [4096, 1024], P(('dp', 'fsdp')), may hold values from -0.09375 to 0.09375
- down_bias: bfloat16 [1024], P(('dp', 'fsdp')), may hold values from -1.5 to 1.5
- norm1_gain: bfloat16 [1024], P(('dp', 'fsdp')), may hold values from 0.099609375 to 1.8984375
- norm1_shift: bfloat16 [1024], P(('dp', 'fsdp')), may hold values from -1.5 to 1.5
- norm2_gain: bfloat16 [1024], P(('dp', 'fsdp')), may hold values from 0.099609375 to 1.8984375
- norm2_shift: bfloat16 [1024], P(('dp', 'fsdp')), may hold values from -1.5 to 1.5
Outputs:
- mixed: bfloat16 [24576, 1024], P(('dp', 'fsdp'))
- input_grad: float32 [24576, 1024], P(('dp', 'fsdp'))
- grad_qkv_weight: float32 [1024, 3072], P(('dp', 'fsdp'))
- grad_query_value_bias: float32 [2048], P(('dp', 'fsdp'))
- grad_dense_weight: float32 [1024, 1024], P(('dp', 'fsdp'))
- grad_dense_bias: float32 [1024], P(('dp', 'fsdp'))
- grad_up_weight: float32 [1024, 4096], P(('dp', 'fsdp'))
- grad_up_bias: float32 [4096], P(('dp', 'fsdp'))
- grad_down_weight: float32 [4096, 1024], P(('dp', 'fsdp'))
- grad_down_bias: float32 [1024], P(('dp', 'fsdp'))
- grad_norm1_gain: float32 [1024], P(('dp', 'fsdp'))
- grad_norm1_shift: float32 [1024], P(('dp', 'fsdp'))
- grad_norm2_gain: float32 [1024], P(('dp', 'fsdp'))
- grad_norm2_shift: float32 [1024], P(('dp', 'fsdp'))
Inputs may be any that keep to these rules, and one draw needn't show every extreme that they name: The 3 lengths of each buffer sum to 384; the largest is exactly 288, so the other two together hold 96 tokens.
All inputs are finite; a program needn't handle non-finite values.
Results may differ from a plain program's by a relative error of at most 0.0095.
Values may be sent and summed in bfloat16 or wider, within the bound.
A program may use at most 256 MiB of HBM per device.

v0:
```python
import math

import jax
import jax.numpy as jnp
from jax import lax
from jax.sharding import PartitionSpec as P

HEADS = 16


epsilon = 1e-05
masked_score = -1e30


def normalize(values, scaling, offset_vec):
    row_mean = jnp.mean(values, axis=-1, keepdims=True)
    centred = values - row_mean
    variance = jnp.mean(centred * centred, axis=-1, keepdims=True)
    return centred * lax.rsqrt(variance + epsilon) * scaling + offset_vec


def gelu_tanh(values):
    return jax.nn.gelu(values, approximate=True)


def across(left_side, right_side):
    return lax.dot_general(
        left_side, right_side, (((0,), (0,)), ((), ())), preferred_element_type=jnp.float32
    )


def against(left_side, right_side):
    return lax.dot_general(
        left_side, right_side, (((1,), (1,)), ((), ())), preferred_element_type=jnp.float32
    )


def attention_masks(lengths_row, block_rows, heads_count):
    positions = jnp.arange(block_rows, dtype=jnp.int32)
    boundaries = jnp.cumsum(lengths_row)
    segments = jnp.sum((positions[:, None] >= boundaries[None, :]).astype(jnp.int32), axis=1)
    visible = (segments[:, None] == segments[None, :]) & (positions[None, :] <= positions[:, None])
    head_slopes = jnp.exp2(-8.0 * jnp.arange(1, heads_count + 1, dtype=jnp.float32) / heads_count)
    distance = (positions[None, :] - positions[:, None]).astype(jnp.float32)
    alibi_bias = head_slopes[:, None, None] * distance[None, :, :]
    return (visible, alibi_bias)


def scores_of(queries, keys_all, visible, alibi_bias, score_scale):
    products = jnp.einsum("qhd,khd->hqk", queries, keys_all, preferred_element_type=jnp.float32)
    return jnp.where(visible[None], products * score_scale + alibi_bias, masked_score)


def fetch(shards):
    collected = (
        lax.all_gather(shards[0], ("dp", "fsdp"), axis=0, tiled=True),
        lax.all_gather(shards[1], ("dp", "fsdp"), axis=0, tiled=True),
        lax.all_gather(shards[2], ("dp", "fsdp"), axis=0, tiled=True),
        lax.all_gather(shards[3], ("dp", "fsdp"), axis=0, tiled=True),
        lax.all_gather(shards[4], ("dp", "fsdp"), axis=0, tiled=True),
        lax.all_gather(shards[5], ("dp", "fsdp"), axis=0, tiled=True),
        lax.all_gather(shards[6], ("dp", "fsdp"), axis=0, tiled=True),
        lax.all_gather(shards[7], ("dp", "fsdp"), axis=0, tiled=True),
        lax.all_gather(shards[8], ("dp", "fsdp"), axis=0, tiled=True),
        lax.all_gather(shards[9], ("dp", "fsdp"), axis=0, tiled=True),
        lax.all_gather(shards[10], ("dp", "fsdp"), axis=0, tiled=True),
        lax.all_gather(shards[11], ("dp", "fsdp"), axis=0, tiled=True),
    )
    return collected


def local(
    tokens,
    lengths,
    cotangent,
    qkv_weight,
    query_value_bias,
    dense_weight,
    dense_bias,
    up_weight,
    up_bias,
    down_weight,
    down_bias,
    norm1_gain,
    norm1_shift,
    norm2_gain,
    norm2_shift,
):
    shards = (
        qkv_weight,
        query_value_bias,
        dense_weight,
        dense_bias,
        up_weight,
        up_bias,
        down_weight,
        down_bias,
        norm1_gain,
        norm1_shift,
        norm2_gain,
        norm2_shift,
    )
    micros = lengths.shape[0]
    block_rows = tokens.shape[0] // micros
    model_width = tokens.shape[1]
    head_dim = model_width // HEADS
    score_scale = 1.0 / math.sqrt(head_dim)
    ranks_total = lax.axis_size("dp") * lax.axis_size("fsdp")
    gradient_sums = [
        jnp.zeros((part.shape[0] * ranks_total,) + part.shape[1:], jnp.float32) for part in shards
    ]
    mixed_parts = []
    input_parts = []
    for micro_index in range(micros):
        row_start = micro_index * block_rows
        inputs = tokens[row_start : row_start + block_rows].astype(jnp.float32)
        visible, alibi_bias = attention_masks(lengths[micro_index], block_rows, HEADS)
        weights = fetch(shards)
        (
            w_qkv,
            b_qv,
            w_dense,
            b_dense,
            w_up,
            b_up,
            w_down,
            b_down,
            gain_one,
            shift_one,
            gain_two,
            shift_two,
        ) = weights
        gain_one = gain_one.astype(jnp.float32)
        shift_one = shift_one.astype(jnp.float32)
        gain_two = gain_two.astype(jnp.float32)
        shift_two = shift_two.astype(jnp.float32)
        b_qv = b_qv.astype(jnp.float32)
        bias_full = jnp.concatenate(
            [b_qv[:model_width], jnp.zeros((model_width,), jnp.float32), b_qv[model_width:]]
        )
        normed_one = normalize(inputs, gain_one, shift_one).astype(jnp.bfloat16)
        projected = (
            jnp.dot(normed_one, w_qkv, preferred_element_type=jnp.float32) + bias_full
        ).astype(jnp.bfloat16)
        queries = projected[:, :model_width].reshape(block_rows, HEADS, head_dim)
        keys_all = projected[:, model_width : 2 * model_width].reshape(block_rows, HEADS, head_dim)
        values_all = projected[:, 2 * model_width :].reshape(block_rows, HEADS, head_dim)
        scores = scores_of(queries, keys_all, visible, alibi_bias, score_scale)
        row_peak = jnp.max(scores, axis=-1, keepdims=True)
        exponent = jnp.exp(scores - row_peak)
        row_total = jnp.sum(exponent, axis=-1, keepdims=True)
        softmaxed = exponent / row_total
        log_total = row_peak + jnp.log(row_total)
        attended = jnp.einsum(
            "hqk,khd->qhd",
            softmaxed.astype(jnp.bfloat16),
            values_all,
            preferred_element_type=jnp.float32,
        )
        attended = attended.reshape(block_rows, model_width).astype(jnp.bfloat16)
        residual_mid = inputs + (
            jnp.dot(attended, w_dense, preferred_element_type=jnp.float32)
            + b_dense.astype(jnp.float32)
        )
        normed_two = normalize(residual_mid, gain_two, shift_two).astype(jnp.bfloat16)
        upper_pre = jnp.dot(normed_two, w_up, preferred_element_type=jnp.float32) + b_up.astype(
            jnp.float32
        )
        activated = gelu_tanh(upper_pre).astype(jnp.bfloat16)
        layer_out = residual_mid + (
            jnp.dot(activated, w_down, preferred_element_type=jnp.float32)
            + b_down.astype(jnp.float32)
        )
        mixed_parts.append(layer_out.astype(jnp.bfloat16))
        weights = fetch(shards)
        (
            w_qkv,
            b_qv,
            w_dense,
            b_dense,
            w_up,
            b_up,
            w_down,
            b_down,
            gain_one,
            shift_one,
            gain_two,
            shift_two,
        ) = weights
        gain_one = gain_one.astype(jnp.float32)
        shift_one = shift_one.astype(jnp.float32)
        gain_two = gain_two.astype(jnp.float32)
        shift_two = shift_two.astype(jnp.float32)
        grad_output = cotangent[row_start : row_start + block_rows]
        grad_float = grad_output.astype(jnp.float32)
        gradient_sums[6] = gradient_sums[6] + across(activated, grad_output)
        gradient_sums[7] = gradient_sums[7] + jnp.sum(grad_float, axis=0)
        grad_activated = against(grad_output, w_down)
        unused_out, gelu_pull = jax.vjp(gelu_tanh, upper_pre)
        grad_upper = gelu_pull(grad_activated)[0]
        gradient_sums[5] = gradient_sums[5] + jnp.sum(grad_upper, axis=0)
        grad_upper_low = grad_upper.astype(jnp.bfloat16)
        gradient_sums[4] = gradient_sums[4] + across(normed_two, grad_upper_low)
        grad_normed_two = against(grad_upper_low, w_up)
        unused_two, norm_pull = jax.vjp(normalize, residual_mid, gain_two, shift_two)
        grad_mid_part, grad_gain_two, grad_shift_two = norm_pull(grad_normed_two)
        gradient_sums[10] = gradient_sums[10] + grad_gain_two
        gradient_sums[11] = gradient_sums[11] + grad_shift_two
        grad_mid = grad_float + grad_mid_part
        gradient_sums[3] = gradient_sums[3] + jnp.sum(grad_mid, axis=0)
        grad_mid_low = grad_mid.astype(jnp.bfloat16)
        gradient_sums[2] = gradient_sums[2] + across(attended, grad_mid_low)
        grad_attended = (
            against(grad_mid_low, w_dense).astype(jnp.bfloat16).reshape(block_rows, HEADS, head_dim)
        )
        scores = scores_of(queries, keys_all, visible, alibi_bias, score_scale)
        softmaxed = jnp.exp(scores - log_total)
        grad_values = jnp.einsum(
            "hqk,qhd->khd",
            softmaxed.astype(jnp.bfloat16),
            grad_attended,
            preferred_element_type=jnp.float32,
        )
        grad_probs = jnp.einsum(
            "qhd,khd->hqk", grad_attended, values_all, preferred_element_type=jnp.float32
        )
        row_inner = jnp.sum(softmaxed * grad_probs, axis=-1, keepdims=True)
        grad_scores = (softmaxed * (grad_probs - row_inner) * score_scale).astype(jnp.bfloat16)
        grad_queries = jnp.einsum(
            "hqk,khd->qhd", grad_scores, keys_all, preferred_element_type=jnp.float32
        )
        grad_keys = jnp.einsum(
            "hqk,qhd->khd", grad_scores, queries, preferred_element_type=jnp.float32
        )
        grad_queries = grad_queries.reshape(block_rows, model_width)
        grad_keys = grad_keys.reshape(block_rows, model_width)
        grad_values = grad_values.reshape(block_rows, model_width)
        gradient_sums[1] = gradient_sums[1] + jnp.concatenate(
            [jnp.sum(grad_queries, axis=0), jnp.sum(grad_values, axis=0)]
        )
        grad_projected_low = jnp.concatenate([grad_queries, grad_keys, grad_values], axis=1).astype(
            jnp.bfloat16
        )
        gradient_sums[0] = gradient_sums[0] + across(normed_one, grad_projected_low)
        grad_normed_one = against(grad_projected_low, w_qkv)
        unused_one, first_pull = jax.vjp(normalize, inputs, gain_one, shift_one)
        grad_in_part, grad_gain_one, grad_shift_one = first_pull(grad_normed_one)
        gradient_sums[8] = gradient_sums[8] + grad_gain_one
        gradient_sums[9] = gradient_sums[9] + grad_shift_one
        input_parts.append(grad_mid + grad_in_part)
    reduced = (
        lax.psum_scatter(gradient_sums[0], ("dp", "fsdp"), scatter_dimension=0, tiled=True),
        lax.psum_scatter(gradient_sums[1], ("dp", "fsdp"), scatter_dimension=0, tiled=True),
        lax.psum_scatter(gradient_sums[2], ("dp", "fsdp"), scatter_dimension=0, tiled=True),
        lax.psum_scatter(gradient_sums[3], ("dp", "fsdp"), scatter_dimension=0, tiled=True),
        lax.psum_scatter(gradient_sums[4], ("dp", "fsdp"), scatter_dimension=0, tiled=True),
        lax.psum_scatter(gradient_sums[5], ("dp", "fsdp"), scatter_dimension=0, tiled=True),
        lax.psum_scatter(gradient_sums[6], ("dp", "fsdp"), scatter_dimension=0, tiled=True),
        lax.psum_scatter(gradient_sums[7], ("dp", "fsdp"), scatter_dimension=0, tiled=True),
        lax.psum_scatter(gradient_sums[8], ("dp", "fsdp"), scatter_dimension=0, tiled=True),
        lax.psum_scatter(gradient_sums[9], ("dp", "fsdp"), scatter_dimension=0, tiled=True),
        lax.psum_scatter(gradient_sums[10], ("dp", "fsdp"), scatter_dimension=0, tiled=True),
        lax.psum_scatter(gradient_sums[11], ("dp", "fsdp"), scatter_dimension=0, tiled=True),
    )
    mixed = jnp.concatenate(mixed_parts, axis=0)
    input_grad = jnp.concatenate(input_parts, axis=0)
    return (
        mixed,
        input_grad,
        reduced[0],
        reduced[1],
        reduced[2],
        reduced[3],
        reduced[4],
        reduced[5],
        reduced[6],
        reduced[7],
        reduced[8],
        reduced[9],
        reduced[10],
        reduced[11],
    )


def solution(mesh):
    placed = (
        P(("dp", "fsdp"), None),
        P(("dp", "fsdp"), None),
        P(("dp", "fsdp"), None),
        P(("dp", "fsdp"), None),
        P(("dp", "fsdp")),
        P(("dp", "fsdp"), None),
        P(("dp", "fsdp")),
        P(("dp", "fsdp"), None),
        P(("dp", "fsdp")),
        P(("dp", "fsdp"), None),
        P(("dp", "fsdp")),
        P(("dp", "fsdp")),
        P(("dp", "fsdp")),
        P(("dp", "fsdp")),
        P(("dp", "fsdp")),
    )
    return jax.shard_map(
        local,
        mesh=mesh,
        in_specs=placed,
        out_specs=(
            P(("dp", "fsdp"), None),
            P(("dp", "fsdp"), None),
            P(("dp", "fsdp"), None),
            P(("dp", "fsdp")),
            P(("dp", "fsdp"), None),
            P(("dp", "fsdp")),
            P(("dp", "fsdp"), None),
            P(("dp", "fsdp")),
            P(("dp", "fsdp"), None),
            P(("dp", "fsdp")),
            P(("dp", "fsdp")),
            P(("dp", "fsdp")),
            P(("dp", "fsdp")),
            P(("dp", "fsdp")),
        ),
        check_vma=False,
    )
```

profile of v0, /device:TPU:0, one launch (start us, length us, event | category | flops | bytes accessed | tf_op | source)
XLA Modules:
  0.0 1375.9 jit_solution(17958464174536437094)
XLA Ops:
  17.0 42.4 %all-reduce.16 = (bf16[2048]{0:T(1024)(128)(2,1)S(1)}, bf16[1024]{0:T(1024)(128)(2,1)S(1)}, bf16[1024]{0:T(1024)(128)(2,1)S(1)}, bf16[1024]{0:T(1024)(128)(2,1)S...) all-reduce(bf16[2048]{0:T(1024)(128)(2,1)S(1)} %dynamic-update-slic, ...), channel_id=1, replica_groups=mesh['dp'=16,'fsdp'=2] {'dp','fsdp'}, use_global_device_ids=true, to_apply=%add.2 | all-reduce | flops 8192 | bytes 32768
  59.4 66.4 %all-gather = bf16[32,1,128]{2,1,0:T(2,128)(2,1)S(1)} all-gather(bf16[1,1,128]{2,1,0:T(2,128)(2,1)} %bitcast.118), channel_id=1, replica_groups=mesh['dp'=16,'fsdp'=2] {'dp','fsdp'}, dimensions={0}, use_global_device_ids=true | all-gather | bytes 8448 | tf_op jit(solution)/shard_map/all_gather | solution.py:61
  130.3 5.9 add_convert_fusion
  142.0 6.3 add_convert_fusion.1
  153.3 4.6 fusion.137
  177.3 43.5 %all-gather.10.cloned.1.call-done = bf16[1024,4096]{1,0:T(8,128)(2,1)} async-done(((bf16[32,4096]{1,0:T(8,128)(2,1)}), bf16[1024,4096]{1,0:T(8,128)(2,1)}) %all-gather.10.cloned.1.call-update) | async-done | bytes 8388624 | tf_op jit(solution)/shard_map/all_gather | solution.py:60
  220.8 10.1 convolution_add_fusion.4
  230.9 68.8 %all-gather.12.cloned.1.call-done = bf16[4096,1024]{1,0:T(8,128)(2,1)} async-done(((bf16[128,1024]{1,0:T(8,128)(2,1)}), bf16[4096,1024]{1,0:T(8,128)(2,1)}) %all-gather.12.cloned.1.call-update) | async-done | bytes 8388624 | tf_op jit(solution)/shard_map/all_gather | solution.py:62
  299.7 11.3 fusion.143
  316.1 6.1 convolution_add_fusion.3
  322.3 11.5 fusion.144
  333.9 7.6 multiply_reduce_fusion.2
  361.6 6.5 fusion.146
  368.1 17.7 %fusion.77 = bf16[16,64,384]{2,1,0:T(8,128)(2,1)} fusion(bf16[384,16,64]{0,2,1:T(8,128)(2,1)} %bitcast.108, f32[16,384,384]{1,2,0:T(8,128)} %fusion.146, f32[16,384,384]{1,2,0:T(8,128)} %copy-done.2, f32[16,384]{1,0:T(8,128)S(1)} %log_add_fusion), kind=kOutput, calls=%fused_computation.127 | convolution fusion | flops 318904704 | bytes 20471808 | tf_op jit(solution)/shard_map/hqk,qhd->khd/dot_general | solution.py:232
  385.8 6.5 fusion.145
  392.3 17.6 %fusion.80 = bf16[16,64,384]{2,1,0:T(8,128)(2,1)} fusion(bf16[384,16,64]{0,2,1:T(8,128)(2,1)} %bitcast.111, f32[16,384,384]{1,2,0:T(8,128)} %fusion.145, f32[16,384,384]{1,2,0:T(8,128)} %copy-done.1, f32[16,384]{1,0:T(8,128)S(1)} %log_add_fusion.1), kind=kOutput, calls=%fused_computation.128 | convolution fusion | flops 318904704 | bytes 20471808 | tf_op jit(solution)/shard_map/hqk,qhd->khd/dot_general | solution.py:232
  409.9 18.2 %bitcast_convert_fusion.1 = (bf16[384,16,64]{0,2,1:T(8,128)(2,1)}, f32[16,64,384]{2,1,0:T(8,128)}) fusion(bf16[384,16,64]{0,2,1:T(8,128)(2,1)} %bitcast.104, f32[16,384,384]{1,2,0:T(8,128)} %fusion.146, f32[16,384,384]{1,2,0:T(8,128)} %copy-done.2, f32[16,384]{1,0:T(8,128)S(1)} %log_add_fusion), kind=kOutput, calls=%fused_computation.103 | convolution fusion | flops 318904704 | bytes 22044672 | tf_op jit(solution)/shard_map/hqk,khd->qhd/dot_general | solution.py:229
  428.1 18.0 %bitcast_convert_fusion.3 = (bf16[384,16,64]{0,2,1:T(8,128)(2,1)}, f32[16,64,384]{2,1,0:T(8,128)}) fusion(bf16[384,16,64]{0,2,1:T(8,128)(2,1)} %bitcast.107, f32[16,384,384]{1,2,0:T(8,128)} %fusion.145, f32[16,384,384]{1,2,0:T(8,128)} %copy-done.1, f32[16,384]{1,0:T(8,128)S(1)} %log_add_fusion.1), kind=kOutput, calls=%fused_computation.107 | convolution fusion | flops 318904704 | bytes 22044672 | tf_op jit(solution)/shard_map/hqk,khd->qhd/dot_general | solution.py:229
  446.1 7.0 bitcast_convert_fusion.2
  453.2 7.1 bitcast_convert_fusion
  464.6 9.8 convolution_add_fusion.2
  474.4 13.8 %fusion.95 = f32[4096,1024]{1,0:T(8,128)} fusion(bf16[768,1024]{1,0:T(8,128)(2,1)} %param.17, f32[384,4096]{1,0:T(8,128)} %convolution_add_fusion.4), kind=kOutput, calls=%fused_computation.143 | convolution fusion | flops 3235381248 | bytes 23855104 | tf_op jit(solution)/shard_map/dot_general | solution.py:27
  488.2 19.3 %convolution_add_fusion = f32[4096,1024]{1,0:T(8,128)} fusion(f32[4096,1024]{1,0:T(8,128)} %fusion.95, bf16[768,1024]{1,0:T(8,128)(2,1)S(1)} %copy-done.10, f32[384,4096]{1,0:T(8,128)} %copy-done.12), kind=kOutput, calls=%fused_computation.24 | convolution fusion | flops 3239575552 | bytes 40632320 | tf_op jit(solution)/shard_map/dot_general | solution.py:27
  507.7 14.1 %fusion.73 = f32[1024,4096]{1,0:T(8,128)} fusion(bf16[384,4096]{1,0:T(8,128)(2,1)} %copy-done.21, f32[384,1024]{1,0:T(8,128)} %copy-done.3, f32[1024]{0:T(1024)S(1)} %convert_element_type.164, f32[1024]{0:T(1024)S(1)} %convert_element_type.163, f32[384]{0:T(512)S(1)} %fusion.107, f32[384]{0:T(512)S(1)} %broadcast_multiply_fusion.2), kind=kOutput, calls=%fused_computation.117 | convolution fusion | flops 3223191552 | bytes 21507072 | tf_op jit(solution)/shard_map/dot_general | solution.py:27
  521.8 12.7 convolution_add_fusion.1
  545.4 6.5 fusion.85
  556.7 41.6 %all-reduce.15 = (f32[2048]{0:T(1024)S(1)}, f32[1024]{0:T(1024)S(1)}, f32[4096]{0:T(1024)S(1)}, f32[1024]{0:T(1024)S(1)}, f32[1024]{0:T(1024)S(1)}, /*index=5*/f...) all-reduce(f32[2048]{0:T(1024)S(1)} %maximum_add_fusion, ...), channel_id=3, replica_groups=mesh['dp'=16,'fsdp'=2] {'dp','fsdp'}, use_global_device_ids=true, to_apply=%region_31.32.clone | all-reduce | flops 12288 | bytes 98304
  603.0 10.2 add_convert_fusion.4
  613.2 9.3 add_convert_fusion.2
  628.6 19.3 %reduce-scatter.5.cloned.1.call-done = f32[32,3072]{1,0:T(8,128)} async-done(((f32[1024,3072]{1,0:T(8,128)}), f32[32,3072]{1,0:T(8,128)}) %reduce-scatter.5.cloned.1.call-update) | async-done | bytes 393232 | tf_op jit(solution)/shard_map/reduce_scatter | solution.py:252
  647.8 359.4 %reduce-scatter.11.cloned.1.call-done = f32[128,1024]{1,0:T(8,128)} async-done(((f32[4096,1024]{1,0:T(8,128)}), f32[128,1024]{1,0:T(8,128)}) %reduce-scatter.11.cloned.1.call-update) | async-done | bytes 524304 | tf_op jit(solution)/shard_map/reduce_scatter | solution.py:258
  1007.3 361.6 %reduce-scatter.9.cloned.1.call-done = f32[32,4096]{1,0:T(8,128)} async-done(((f32[1024,4096]{1,0:T(8,128)}), f32[32,4096]{1,0:T(8,128)}) %reduce-scatter.9.cloned.1.call-update) | async-done | bytes 524304 | tf_op jit(solution)/shard_map/reduce_scatter | solution.py:256
  (252 shorter events, 99.6 us)
Async XLA Ops:
  7.2 121.5 %copy-start = (bf16[768,1024]{1,0:T(8,128)(2,1)S(1)}, bf16[768,1024]{1,0:T(8,128)(2,1)}, u32[]{:S(2)}) copy-start(bf16[768,1024]{1,0:T(8,128)(2,1)} %param.15) | copy-start | bytes 4718596
  7.2 122.9 %all-gather.6.cloned.1.call-start = ((), (), s32[]{:S(2)}) async-start(), calls=%async_computation.4 | async-start | bytes 6488064 | tf_op jit(solution)/shard_map/all_gather | solution.py:56
  7.9 155.5 %all-gather.8.cloned.1.call-start = ((), (), s32[]{:S(2)}) async-start(), calls=%async_computation.5 | async-start | bytes 2162688 | tf_op jit(solution)/shard_map/all_gather | solution.py:58
  8.7 212.1 %all-gather.10.cloned.1.call-start = ((), (), s32[]{:S(2)}) async-start(), calls=%async_computation.6 | async-start | bytes 8650752 | tf_op jit(solution)/shard_map/all_gather | solution.py:60
  9.4 290.3 %all-gather.12.cloned.1.call-start = ((), (), s32[]{:S(2)}) async-start(), calls=%async_computation.7 | async-start | bytes 8650752 | tf_op jit(solution)/shard_map/all_gather | solution.py:62
  10.0 618.6 %reduce-scatter.7.cloned.1.call-start = ((), (), s32[]{:S(2)}) async-start(), calls=%async_computation.9 | async-start | bytes 4325376 | tf_op jit(solution)/shard_map/reduce_scatter | solution.py:254
  59.4 82.6 %copy-start.32 = (f32[1024]{0:T(1024)}, f32[1024]{0:T(1024)S(1)}, u32[]{:S(2)}) copy-start(f32[1024]{0:T(1024)S(1)} %convert_element_type.151) | copy-start | bytes 12292
  59.4 82.6 %copy-start.42 = (f32[1024]{0:T(1024)}, f32[1024]{0:T(1024)S(1)}, u32[]{:S(2)}) copy-start(f32[1024]{0:T(1024)S(1)} %convert_element_type.152) | copy-start | bytes 12292
  128.6 13.4 copy-start.45
  129.2 12.8 copy-start.47
  299.7 13.0 copy-start.59
  322.3 11.6 copy-start.12
  322.3 11.6 copy-start.4
  333.8 7.7 copy-start.22
  347.9 300.0 %reduce-scatter.5.cloned.1.call-start = ((), (), s32[]{:S(2)}) async-start(), calls=%async_computation.8 | async-start | bytes 12976128 | tf_op jit(solution)/shard_map/reduce_scatter | solution.py:252
  446.1 7.0 copy-start.14
  453.1 7.2 copy-start.24
  453.1 7.2 copy-start.33
  453.1 7.2 copy-start.34
  453.1 7.2 copy-start.36
  453.1 7.2 copy-start.43
  453.2 7.2 copy-start.46
  453.2 7.1 copy-start.48
  474.4 532.9 %reduce-scatter.11.cloned.1.call-start = ((), (), s32[]{:S(2)}) async-start(), calls=%async_computation.11 | async-start | bytes 17301504 | tf_op jit(solution)/shard_map/reduce_scatter | solution.py:258
  474.4 13.8 %copy-start.10 = (bf16[768,1024]{1,0:T(8,128)(2,1)S(1)}, bf16[768,1024]{1,0:T(8,128)(2,1)}, u32[]{:S(2)}) copy-start(bf16[768,1024]{1,0:T(8,128)(2,1)} %param.17) | copy-start | bytes 4718596
  507.5 861.4 %reduce-scatter.9.cloned.1.call-start = ((), (), s32[]{:S(2)}) async-start(), calls=%async_computation.10 | async-start | bytes 17301504 | tf_op jit(solution)/shard_map/reduce_scatter | solution.py:256
  507.7 14.1 %copy-start.23 = (bf16[384,4096]{1,0:T(8,128)(2,1)S(1)}, bf16[384,4096]{1,0:T(8,128)(2,1)}, u32[]{:S(2)}) copy-start(bf16[384,4096]{1,0:T(8,128)(2,1)} %copy-done.22) | copy-start | bytes 9437188
  535.2 6.9 copy-start.57
  542.2 9.8 slice-start
  613.2 10.7 copy-start.11
  613.2 10.7 copy-start.16
  613.2 10.7 copy-start.18
  (38 other events, 119.2 us)
Sparse Core Ops, SparseCore 0:
  10.9 72.5 all-gather.5
  86.5 54.9 all-gather.7
  144.5 76.2 all-gather.9
  223.7 75.9 all-gather.11
  348.0 140.6 reduce-scatter.6
  495.1 152.7 reduce-scatter.4
  650.8 356.4 reduce-scatter.10
  1010.2 358.5 reduce-scatter.8
where the time goes:
time: 1380 us
  waiting for transfers between devices  855 us (62%)
  matrix products  293 us (21%)
  blocking collectives  150 us (11%)
  local copies, waits for them, and re-layouts  37 us (3%)
  other arithmetic  24.3 us (2%)
  between operations  15.5 us (1%)
    reduce_scatter x1, waiting for transfers between devices, local(): lax.psum_scatter(gradient_sums[4], ('dp', 'fsdp'), scatter_dimension=0, t...  362 us
    reduce_scatter x1, waiting for transfers between devices, local(): lax.psum_scatter(gradient_sums[6], ('dp', 'fsdp'), scatter_dimension=0, t...  359 us
    unnamed x2, blocking collectives  84 us
    dot_general x8, matrix products, across(): lax.dot_general(left_side, right_side, (((0,), (0,)), ((), ())), preferre...  78.6 us
    all_gather x1, waiting for transfers between devices, fetch(): lax.all_gather(shards[6], ('dp', 'fsdp'), axis=0, tiled=True)  68.8 us
    all_gather x1, blocking collectives, fetch(): lax.all_gather(shards[5], ('dp', 'fsdp'), axis=0, tiled=True)  66.4 us
    dot_general x8, matrix products, against(): lax.dot_general(left_side, right_side, (((1,), (1,)), ((), ())), preferre...  52.1 us
    all_gather x1, waiting for transfers between devices, fetch(): lax.all_gather(shards[4], ('dp', 'fsdp'), axis=0, tiled=True)  43.5 us
  transfers between devices with their start and end apart: 8, of which 5 were waited for; matrix products, arithmetic and copies ran while one was open for 22% of the time, Pallas kernels for 0%

commit v1 on v0

v1 whole, which is shorter than its diff:
```python
import functools
import math

import jax
import jax.numpy as jnp
from jax import lax
from jax.experimental import pallas as pl
from jax.experimental.pallas import tpu as pltpu
from jax.sharding import PartitionSpec as P

HEADS = 16
AXES = ("dp", "fsdp")
TILE = 128

epsilon = 1e-05
far_away = -1e33


def normalize(values, scaling, offset_vec):
    row_mean = jnp.mean(values, axis=-1, keepdims=True)
    centred = values - row_mean
    variance = jnp.mean(centred * centred, axis=-1, keepdims=True)
    return centred * lax.rsqrt(variance + epsilon) * scaling + offset_vec


def gelu_tanh(values):
    return jax.nn.gelu(values, approximate=True)


def across(left_side, right_side):
    return lax.dot_general(
        left_side, right_side, (((0,), (0,)), ((), ())), preferred_element_type=jnp.float32
    )


def against(left_side, right_side):
    return lax.dot_general(
        left_side, right_side, (((1,), (1,)), ((), ())), preferred_element_type=jnp.float32
    )


def device_bits():
    fsdp_bits = (lax.axis_size("fsdp") - 1).bit_length()
    total_bits = (lax.axis_size("dp") * lax.axis_size("fsdp") - 1).bit_length()
    inner = list(range(fsdp_bits))
    core = fsdp_bits
    outer = list(range(fsdp_bits + 1, total_bits))
    return inner, core, outer, total_bits


def swap(piece, bit, count):
    return lax.ppermute(piece, AXES, [(i, i ^ (1 << bit)) for i in range(count)])


def gather(shard, order):
    count = lax.axis_size("dp") * lax.axis_size("fsdp")
    bits = (count - 1).bit_length()
    index = lax.axis_index(AXES)
    held = shard.reshape((1,) * bits + shard.shape)
    for bit in order:
        axis = bits - 1 - bit
        got = swap(held, bit, count)
        upper = ((index >> bit) & 1) == 1
        held = jnp.concatenate(
            [jnp.where(upper, got, held), jnp.where(upper, held, got)], axis=axis
        )
    return held.reshape((count * shard.shape[0],) + shard.shape[1:])


def scatter_sum(whole, order, link_type):
    count = lax.axis_size("dp") * lax.axis_size("fsdp")
    bits = (count - 1).bit_length()
    index = lax.axis_index(AXES)
    held = whole.reshape((2,) * bits + (whole.shape[0] // count,) + whole.shape[1:])
    for step, bit in enumerate(order):
        axis = bits - 1 - bit
        mine = (index >> bit) & 1
        kept = lax.dynamic_slice_in_dim(held, mine, 1, axis)
        given = lax.dynamic_slice_in_dim(held, 1 - mine, 1, axis)
        got = swap(given.astype(link_type), bit, count)
        held = kept.astype(jnp.float32) + got.astype(jnp.float32)
        if step + 1 < len(order):
            held = held.astype(link_type)
    return held.reshape((whole.shape[0] // count,) + whole.shape[1:])


def distances(lengths_ref, buffer, rows):
    first = lengths_ref[buffer, 0]
    second = first + lengths_ref[buffer, 1]
    row = lax.broadcasted_iota(jnp.int32, (rows, rows), 0)
    col = lax.broadcasted_iota(jnp.int32, (rows, rows), 1)
    row_part = (row >= first).astype(jnp.int32) + (row >= second).astype(jnp.int32)
    col_part = (col >= first).astype(jnp.int32) + (col >= second).astype(jnp.int32)
    seen = (row_part == col_part) & (col <= row)
    return jnp.where(seen, (col - row).astype(jnp.float32), far_away)


def attend_kernel(lengths_ref, slopes_ref, q_ref, k_ref, v_ref, out_ref, probs_ref, far_ref):
    rows, width = q_ref.shape
    buffer, pair = pl.program_id(0), pl.program_id(1)

    @pl.when(pair == 0)
    def _():
        far_ref[...] = distances(lengths_ref, buffer, rows)

    lane = lax.broadcasted_iota(jnp.int32, (TILE, width), 1)
    low_half = lane < width // 2
    scale = 1.0 / math.sqrt(width // 2)
    for start in range(0, rows, TILE):
        stop = start + TILE
        q = q_ref[start:stop, :] * scale
        q = q.astype(jnp.bfloat16)
        results = []
        for head in range(2):
            picked = jnp.where(low_half == (head == 0), q, jnp.zeros_like(q))
            scores = against(picked, k_ref[:stop, :])
            scores = scores + slopes_ref[2 * pair + head] * far_ref[start:stop, :stop]
            peak = jnp.max(scores, axis=-1, keepdims=True)
            exponent = jnp.exp(scores - peak)
            total = jnp.sum(exponent, axis=-1, keepdims=True)
            probs = (exponent * (1.0 / total)).astype(jnp.bfloat16)
            probs_ref[0, head, start:stop, :stop] = probs
            results.append(
                jnp.dot(probs, v_ref[:stop, :], preferred_element_type=jnp.float32)
            )
        out_ref[start:stop, :] = jnp.where(low_half, results[0], results[1]).astype(jnp.bfloat16)


def attend(projected, lengths, slopes):
    rows, buffers = projected.shape[0], lengths.shape[0]
    block, width = rows // buffers, projected.shape[1] // 3
    pairs = HEADS // 2
    pair_width = width // pairs
    spec = lambda part: pl.BlockSpec((block, pair_width), lambda b, p: (b, part * pairs + p))
    smem = pl.BlockSpec(memory_space=pltpu.SMEM)
    return pl.pallas_call(
        attend_kernel,
        grid=(buffers, pairs),
        in_specs=[smem, smem, spec(0), spec(1), spec(2)],
        out_specs=[
            spec(0),
            pl.BlockSpec((1, 2, block, block), lambda b, p: (b, p, 0, 0)),
        ],
        out_shape=[
            jax.ShapeDtypeStruct((rows, width), jnp.bfloat16),
            jax.ShapeDtypeStruct((buffers, HEADS, block, block), jnp.bfloat16),
        ],
        scratch_shapes=[pltpu.VMEM((block, block), jnp.float32)],
        compiler_params=pltpu.CompilerParams(vmem_limit_bytes=32 * 2**20),
        cost_estimate=pl.CostEstimate(
            flops=4 * rows * block * width, bytes_accessed=16 * 2**20, transcendentals=0
        ),
    )(lengths, slopes, projected, projected, projected)


def attend_back_kernel(
    g_ref, probs_ref, q_ref, k_ref, v_ref, gq_ref, gk_ref, gv_ref, sums_ref, gk_sum, gv_sum
):
    rows, width = q_ref.shape
    scale = 1.0 / math.sqrt(width // 2)
    low_half = lax.broadcasted_iota(jnp.int32, (TILE, width), 1) < width // 2
    q_total = jnp.zeros((1, width), jnp.float32)
    gk_sum[...] = jnp.zeros_like(gk_sum)
    gv_sum[...] = jnp.zeros_like(gv_sum)
    for start in range(0, rows, TILE):
        stop = start + TILE
        g = g_ref[start:stop, :]
        q = (q_ref[start:stop, :] * scale).astype(jnp.bfloat16)
        gq = []
        for head in range(2):
            here = low_half == (head == 0)
            g_here = jnp.where(here, g, jnp.zeros_like(g))
            q_here = jnp.where(here, q, jnp.zeros_like(q))
            probs_low = probs_ref[0, head, start:stop, :stop]
            probs = probs_low.astype(jnp.float32)
            grad_probs = against(g_here, v_ref[:stop, :])
            inner = jnp.sum(probs * grad_probs, axis=-1, keepdims=True)
            grad_scores = (probs * (grad_probs - inner)).astype(jnp.bfloat16)
            gq.append(jnp.dot(grad_scores, k_ref[:stop, :], preferred_element_type=jnp.float32))
            gk_sum[:stop, :] += across(grad_scores, q_here)
            gv_sum[:stop, :] += across(probs_low, g_here)
        gq_block = jnp.where(low_half, gq[0], gq[1]) * scale
        q_total += jnp.sum(gq_block, axis=0, keepdims=True)
        gq_ref[start:stop, :] = gq_block.astype(jnp.bfloat16)
    gk_ref[...] = gk_sum[...].astype(jnp.bfloat16)
    gv_ref[...] = gv_sum[...].astype(jnp.bfloat16)
    sums_ref[0, 0:1, :] = q_total
    sums_ref[0, 1:2, :] = jnp.sum(gv_sum[...], axis=0, keepdims=True)


def attend_back(grad_attended, probs, projected):
    rows, buffers = projected.shape[0], probs.shape[0]
    block, width = rows // buffers, projected.shape[1] // 3
    pairs = HEADS // 2
    pair_width = width // pairs
    spec = lambda part: pl.BlockSpec((block, pair_width), lambda b, p: (b, part * pairs + p))
    flat = jax.ShapeDtypeStruct((rows, width), jnp.bfloat16)
    return pl.pallas_call(
        attend_back_kernel,
        grid=(buffers, pairs),
        in_specs=[
            spec(0),
            pl.BlockSpec((1, 2, block, block), lambda b, p: (b, p, 0, 0)),
            spec(0),
            spec(1),
            spec(2),
        ],
        out_specs=[
            spec(0),
            spec(0),
            spec(0),
            pl.BlockSpec((1, 2, pair_width), lambda b, p: (b, 0, p)),
        ],
        out_shape=[flat, flat, flat, jax.ShapeDtypeStruct((buffers, 2, width), jnp.float32)],
        scratch_shapes=[pltpu.VMEM((block, pair_width), jnp.float32)] * 2,
        compiler_params=pltpu.CompilerParams(vmem_limit_bytes=32 * 2**20),
        cost_estimate=pl.CostEstimate(
            flops=10 * rows * block * width, bytes_accessed=20 * 2**20, transcendentals=0
        ),
    )(grad_attended, probs, projected, projected, projected)


def local(
    tokens,
    lengths,
    cotangent,
    qkv_weight,
    query_value_bias,
    dense_weight,
    dense_bias,
    up_weight,
    up_bias,
    down_weight,
    down_bias,
    norm1_gain,
    norm1_shift,
    norm2_gain,
    norm2_shift,
):
    width = tokens.shape[1]
    inner, core, outer, bits = device_bits()
    outer_down = outer[::-1]
    gather_a = outer_down + inner[::-1] + [core]
    gather_b = outer_down[:-1] + inner[::-1] + outer_down[-1:] + [core]
    scatter_a, scatter_b = gather_a[::-1], gather_b[::-1]
    count = 1 << bits

    small = (
        query_value_bias,
        dense_bias,
        up_bias,
        down_bias,
        norm1_gain,
        norm1_shift,
        norm2_gain,
        norm2_shift,
    )
    sizes = [part.shape[0] for part in small]
    offsets = [sum(sizes[:i]) for i in range(len(sizes))]
    packed = gather(jnp.concatenate(small).reshape(1, -1), gather_b).astype(jnp.float32)
    b_qv, b_dense, b_up, b_down, gain_one, shift_one, gain_two, shift_two = [
        packed[:, at : at + size].reshape(-1) for at, size in zip(offsets, sizes)
    ]
    w_qkv = gather(qkv_weight, gather_a)
    w_dense = gather(dense_weight, gather_b)
    w_up = gather(up_weight, gather_a)
    w_down = gather(down_weight, gather_b)

    slopes = jnp.exp2(-8.0 * jnp.arange(1, HEADS + 1, dtype=jnp.float32) / HEADS)
    inputs = tokens.astype(jnp.float32)
    bias_full = jnp.concatenate([b_qv[:width], jnp.zeros((width,), jnp.float32), b_qv[width:]])
    normed_one = normalize(inputs, gain_one, shift_one).astype(jnp.bfloat16)
    projected = (
        jnp.dot(normed_one, w_qkv, preferred_element_type=jnp.float32) + bias_full
    ).astype(jnp.bfloat16)
    attended, probs = attend(projected, lengths, slopes)
    residual_mid = inputs + (
        jnp.dot(attended, w_dense, preferred_element_type=jnp.float32) + b_dense
    )
    normed_two = normalize(residual_mid, gain_two, shift_two).astype(jnp.bfloat16)
    upper_pre = jnp.dot(normed_two, w_up, preferred_element_type=jnp.float32) + b_up
    activated = gelu_tanh(upper_pre).astype(jnp.bfloat16)
    layer_out = residual_mid + (
        jnp.dot(activated, w_down, preferred_element_type=jnp.float32) + b_down
    )
    mixed = layer_out.astype(jnp.bfloat16)

    grad_float = cotangent.astype(jnp.float32)
    grad_down_weight = scatter_sum(
        across(activated, cotangent).astype(jnp.bfloat16), scatter_a, jnp.bfloat16
    )
    grad_down_bias = jnp.sum(grad_float, axis=0)
    grad_activated = against(cotangent, w_down)
    grad_upper = jax.vjp(gelu_tanh, upper_pre)[1](grad_activated)[0]
    grad_up_bias = jnp.sum(grad_upper, axis=0)
    grad_upper_low = grad_upper.astype(jnp.bfloat16)
    grad_up_weight = scatter_sum(
        across(normed_two, grad_upper_low).astype(jnp.bfloat16), scatter_b, jnp.bfloat16
    )
    grad_normed_two = against(grad_upper_low, w_up)
    grad_mid_part, grad_gain_two, grad_shift_two = jax.vjp(
        normalize, residual_mid, gain_two, shift_two
    )[1](grad_normed_two)
    grad_mid = grad_float + grad_mid_part
    grad_dense_bias = jnp.sum(grad_mid, axis=0)
    grad_mid_low = grad_mid.astype(jnp.bfloat16)
    grad_dense_weight = scatter_sum(
        across(attended, grad_mid_low).astype(jnp.bfloat16), scatter_a, jnp.bfloat16
    )
    grad_attended = against(grad_mid_low, w_dense).astype(jnp.bfloat16)
    grad_q, grad_k, grad_v, bias_sums = attend_back(grad_attended, probs, projected)
    grad_qv_bias = jnp.sum(bias_sums, axis=0).reshape(-1)
    grad_projected_low = jnp.concatenate([grad_q, grad_k, grad_v], axis=1)
    grad_qkv_weight = scatter_sum(
        across(normed_one, grad_projected_low).astype(jnp.bfloat16), scatter_b, jnp.bfloat16
    )
    grad_normed_one = against(grad_projected_low, w_qkv)
    grad_in_part, grad_gain_one, grad_shift_one = jax.vjp(
        normalize, inputs, gain_one, shift_one
    )[1](grad_normed_one)
    input_grad = grad_mid + grad_in_part

    small_grads = (
        grad_qv_bias,
        grad_dense_bias,
        grad_up_bias,
        grad_down_bias,
        grad_gain_one,
        grad_shift_one,
        grad_gain_two,
        grad_shift_two,
    )
    summed = scatter_sum(
        jnp.concatenate([part.reshape(count, -1) for part in small_grads], axis=1),
        scatter_a,
        jnp.float32,
    ).reshape(-1)
    (g_qv, g_dense, g_up, g_down, g_gain_one, g_shift_one, g_gain_two, g_shift_two) = [
        summed[at : at + size] for at, size in zip(offsets, sizes)
    ]
    return (
        mixed,
        input_grad,
        grad_qkv_weight,
        g_qv,
        grad_dense_weight,
        g_dense,
        grad_up_weight,
        g_up,
        grad_down_weight,
        g_down,
        g_gain_one,
        g_shift_one,
        g_gain_two,
        g_shift_two,
    )


def solution(mesh):
    rows, vector = P(AXES, None), P(AXES)
    return jax.shard_map(
        local,
        mesh=mesh,
        in_specs=(rows, rows, rows, rows, vector, rows, vector, rows, vector, rows)
        + (vector,) * 5,
        out_specs=(rows, rows, rows, vector, rows, vector, rows, vector, rows, vector)
        + (vector,) * 4,
        check_vma=False,
    )
```

time: 1380 us -> 630 us (0.46)
  waiting for transfers between devices: 855 us -> 261 us
  matrix products: 293 us -> 119 us
  blocking collectives: 150 us -> 0 us
  Pallas kernels: 0 us -> 72.9 us
  other arithmetic: 24.3 us -> 87.1 us
  starting transfers between devices: 0.95 us -> 53.1 us
    reduce_scatter x4 -> x0, waiting for transfers between devices: 740 us -> none  [the longest x1 362 us: local(): lax.psum_scatter(gradient_sums[4], ('dp', 'fsdp'), scatter_dimension=0, t...]
    ppermute x0 -> x50, waiting for transfers between devices: none -> 261 us  [swap(): return lax.ppermute(piece, AXES, [(i, i ^ 1 << bit) for i in range(count)])]
    dot_general x18 -> x3, matrix products: 150 us -> 30.7 us  [the longest x1 15 us: local(): jnp.dot(activated, w_down, preferred_element_type=jnp.float32) + b_down]
    all_gather x4 -> x0, waiting for transfers between devices: 112 us -> none  [the longest x1 68.8 us: fetch(): lax.all_gather(shards[6], ('dp', 'fsdp'), axis=0, tiled=True)]
    unnamed x2 -> x0, blocking collectives: 84 us -> none
    pallas_call x0 -> x2, Pallas kernels: none -> 72.9 us  [the longest x1 36.5 us: attend_back(): pl.pallas_call(attend_back_kernel, grid=(buffers, pairs), in_specs=[spec(...]
    all_gather x1 -> x0, blocking collectives: 66.4 us -> none  [fetch(): lax.all_gather(shards[5], ('dp', 'fsdp'), axis=0, tiled=True)]
    ppermute x0 -> x50, starting transfers between devices: none -> 53.1 us  [swap(): return lax.ppermute(piece, AXES, [(i, i ^ 1 << bit) for i in range(count)])]
  transfers between devices with their start and end apart: 8 -> 50, of which waited for: 5 -> 30; matrix products, arithmetic and copies ran while one was open for 22% -> 18% of each run, Pallas kernels for 0% -> 6%
where the time goes in v1:
time: 630 us; the launch traced here: 623 us
  waiting for transfers between devices  261 us (41%)
  matrix products  119 us (19%)
  other arithmetic  87.1 us (14%)
  Pallas kernels  72.9 us (12%)
  starting transfers between devices  53.1 us (8%)
  local copies, waits for them, and re-layouts  27.3 us (4%)
    ppermute x50, waiting for transfers between devices, swap(): return lax.ppermute(piece, AXES, [(i, i ^ 1 << bit) for i in range(count)])  261 us
    ppermute x50, starting transfers between devices, swap(): return lax.ppermute(piece, AXES, [(i, i ^ 1 << bit) for i in range(count)])  53.1 us
    dot_general x4, matrix products, against(): lax.dot_general(left_side, right_side, (((1,), (1,)), ((), ())), preferre...  42 us
    dot_general x4, matrix products, across(): lax.dot_general(left_side, right_side, (((0,), (0,)), ((), ())), preferre...  37.7 us
    pallas_call x1, Pallas kernels, attend_back(): pl.pallas_call(attend_back_kernel, grid=(buffers, pairs), in_specs=[spec(...  36.5 us
    pallas_call x1, Pallas kernels, attend(): pl.pallas_call(attend_kernel, grid=(buffers, pairs), in_specs=[smem, smem...  36.4 us
    concatenate x24, other arithmetic, gather(): jnp.concatenate([jnp.where(upper, got, held), jnp.where(upper, held, got)...  33.8 us
    select_n x25, other arithmetic, gather(): jnp.where(upper, got, held)  22 us
  transfers between devices with their start and end apart: 50, of which 30 were waited for; matrix products, arithmetic and copies ran while one was open for 18% of the time, Pallas kernels for 6%

profile of v1, /device:TPU:0, one launch (start us, length us, event | category | flops | bytes accessed | tf_op | source)
XLA Modules:
  0.0 622.9 jit_solution(12837712151228679927)
XLA Ops:
  19.5 8.0 %collective-permute-done.1 = bf16[2,1,1,1,1,1,384]{6,5,4,3,2,1,0:T(2,128)(2,1)S(1)} collective-permute-done((bf16[2,1,1,1,1,1,384]{6,5,4,3,2,1,0:T(2,128)(2,1)S(1)}, bf16[2,1,1,1,1,1,384]{6,5,4,3,2,1,0:T(2,128)(2,1)S(1)}, u32[]{:S(2)}, u32[]{:S(2)}) %collective-permute-start.1) | collective-permute-done | bytes 1568 | tf_op jit(solution)/shard_map/ppermute | solution.py:52
  39.4 10.6 %collective-permute-done.11 = bf16[2,1,1,1,1,32,1024]{6,5,4,3,2,1,0:T(8,128)(2,1)S(1)} collective-permute-done((bf16[2,1,1,1,1,32,1024]{6,5,4,3,2,1,0:T(8,128)(2,1)S(1)}, bf16[2,1,1,1,1,32,1024]{6,5,4,3,2,1,0:T(8,128)(2,1)S(1)}, u32[]{:S(2)}, u32[]{:S(2)}) %collective-permute-start.11) | collective-permute-done | bytes 131104 | tf_op jit(solution)/shard_map/ppermute | solution.py:52
  65.5 9.5 %collective-permute-done.21 = bf16[2,1,1,1,1,128,1024]{6,5,4,3,2,1,0:T(8,128)(2,1)S(1)} collective-permute-done((bf16[2,1,1,1,1,128,1024]{6,5,4,3,2,1,0:T(8,128)(2,1)S(1)}, bf16[2,1,1,1,1,128,1024]{6,5,4,3,2,1,0:T(8,128)(2,1)S(1)}, u32[]{:S(2)}, u32[]{:S(2)}) %collective-permute-start.21) | collective-permute-done | bytes 524320 | tf_op jit(solution)/shard_map/ppermute | solution.py:52
  75.8 9.2 %collective-permute-done.16 = bf16[2,1,1,1,1,32,4096]{6,5,4,3,2,1,0:T(8,128)(2,1)S(1)} collective-permute-done((bf16[2,1,1,1,1,32,4096]{6,5,4,3,2,1,0:T(8,128)(2,1)S(1)}, bf16[2,1,1,1,1,32,4096]{6,5,4,3,2,1,0:T(8,128)(2,1)S(1)}, u32[]{:S(2)}, u32[]{:S(2)}) %collective-permute-start.16) | collective-permute-done | bytes 524320 | tf_op jit(solution)/shard_map/ppermute | solution.py:52
  92.1 9.3 %collective-permute-done.22 = bf16[2,2,1,1,1,128,1024]{6,5,4,3,2,1,0:T(8,128)(2,1)S(1)} collective-permute-done((bf16[2,2,1,1,1,128,1024]{6,5,4,3,2,1,0:T(8,128)(2,1)S(1)}, bf16[2,2,1,1,1,128,1024]{6,5,4,3,2,1,0:T(8,128)(2,1)S(1)}, u32[]{:S(2)}, u32[]{:S(2)}) %collective-permute-start.22) | collective-permute-done | bytes 1048608 | tf_op jit(solution)/shard_map/ppermute | solution.py:52
  104.7 7.9 %collective-permute-done.17 = bf16[2,2,1,1,1,32,4096]{6,5,4,3,2,1,0:T(8,128)(2,1)S(1)} collective-permute-done((bf16[2,2,1,1,1,32,4096]{6,5,4,3,2,1,0:T(8,128)(2,1)S(1)}, bf16[2,2,1,1,1,32,4096]{6,5,4,3,2,1,0:T(8,128)(2,1)S(1)}, u32[]{:S(2)}, u32[]{:S(2)}) %collective-permute-start.17) | collective-permute-done | bytes 1048608 | tf_op jit(solution)/shard_map/ppermute | solution.py:52
  116.1 19.0 %collective-permute-done.8 = bf16[2,2,2,1,1,32,3072]{6,5,4,3,2,1,0:T(8,128)(2,1)S(1)} collective-permute-done((bf16[2,2,2,1,1,32,3072]{6,5,4,3,2,1,0:T(8,128)(2,1)S(1)}, bf16[2,2,2,1,1,32,3072]{6,5,4,3,2,1,0:T(8,128)(2,1)S(1)}, u32[]{:S(2)}, u32[]{:S(2)}) %collective-permute-start.8) | collective-permute-done | bytes 1572896 | tf_op jit(solution)/shard_map/ppermute | solution.py:52
  141.8 14.2 %collective-permute-done.23 = bf16[2,2,1,1,2,128,1024]{6,5,4,3,2,1,0:T(8,128)(2,1)} collective-permute-done((bf16[2,2,1,1,2,128,1024]{6,5,4,3,2,1,0:T(8,128)(2,1)}, bf16[2,2,1,1,2,128,1024]{6,5,4,3,2,1,0:T(8,128)(2,1)}, u32[]{:S(2)}, u32[]{:S(2)}) %collective-permute-start.23) | collective-permute-done | bytes 2097184 | tf_op jit(solution)/shard_map/ppermute | solution.py:52
  160.3 16.6 %collective-permute-done.18 = bf16[2,2,2,1,1,32,4096]{6,5,4,3,2,1,0:T(8,128)(2,1)} collective-permute-done((bf16[2,2,2,1,1,32,4096]{6,5,4,3,2,1,0:T(8,128)(2,1)}, bf16[2,2,2,1,1,32,4096]{6,5,4,3,2,1,0:T(8,128)(2,1)}, u32[]{:S(2)}, u32[]{:S(2)}) %collective-permute-start.18) | collective-permute-done | bytes 2097184 | tf_op jit(solution)/shard_map/ppermute | solution.py:52
  190.4 8.4 %add_convert_fusion.q_ref.k_ref.v_ref = bf16[768,3072]{1,0:T(8,128)(2,1)S(1)} fusion(bf16[1024,3072]{1,0:T(8,128)(2,1)} %bitcast.88, f32[3072]{0:T(1024)S(1)} %pad_maximum_fusion.22, bf16[768,1024]{1,0:T(8,128)(2,1)S(1)} %copy-done.2, f32[1024]{0:T(1024)S(1)} %add.269, f32[1024]{0:T(1024)S(1)} %mul.184, f32[768]{0:T(1024)S(1)} %fusion.28, ...), kind=kOutput, calls=%fused_computation.14 | convolution fusion | flops 4841275392 | bytes 12609536 | tf_op jit(solution)/shard_map/dot_general | solution.py:274
  198.9 36.4 %shard_map.254 = (bf16[768,1024]{1,0:T(8,128)(2,1)S(1)}, bf16[2,16,384,384]{3,2,1,0:T(8,128)(2,1)S(1)}) custom-call(s32[2,3]{1,0:T(2,128)S(1)} %copy-done.1, f32[16]{0:T(128)S(1)} %multiply_exponential_fusion.slopes_ref, bf16[768,3072]{1,0:T(8,128)(2,1)S(1)} %add_convert_fusion.q_ref.k_ref.v_ref, bf16[768,3072]{1,0:T(8,128)(2,1)S(1)} %add_convert_fusion.q_ref.k_ref.v_ref, ...), custom_call_target="tpu_custom_call" | custom-call | flops 1207959552 | bytes 16777216 | tf_op jit(solution)/shard_map/pallas_call | solution.py:136
  245.2 7.6 %pad_maximum_fusion.1 = bf16[2,2,2,2,2,128,1024]{6,5,4,3,2,1,0:T(8,128)(2,1)} fusion(bf16[2,2,2,1,2,128,1024]{6,5,4,3,2,1,0:T(8,128)(2,1)} %get-tuple-element.40, bf16[2,2,2,1,2,128,1024]{6,5,4,3,2,1,0:T(8,128)(2,1)} %get-tuple-element.39), kind=kLoop, calls=%fused_computation.16 | loop fusion | flops 4194304 | bytes 16777216 | tf_op jit(solution)/shard_map/concatenate | solution.py:64
  258.4 7.5 %pad_maximum_fusion = bf16[2,2,2,2,2,32,4096]{6,5,4,3,2,1,0:T(8,128)(2,1)} fusion(bf16[2,2,2,1,2,32,4096]{6,5,4,3,2,1,0:T(8,128)(2,1)} %get-tuple-element.38, bf16[2,2,2,1,2,32,4096]{6,5,4,3,2,1,0:T(8,128)(2,1)} %get-tuple-element.37), kind=kLoop, calls=%fused_computation.15 | loop fusion | flops 4194304 | bytes 16777216 | tf_op jit(solution)/shard_map/concatenate | solution.py:64
  265.9 13.8 %fusion.35 = f32[768,4096]{1,0:T(8,128)} fusion(bf16[1024,4096]{1,0:T(8,128)(2,1)} %bitcast.86, f32[768,1024]{1,0:T(8,128)} %copy-done.8, f32[1024]{0:T(1024)S(1)} %add.279, f32[1024]{0:T(1024)S(1)} %mul.190, f32[768]{0:T(1024)S(1)} %fusion.29, f32[768]{0:T(1024)S(1)} %broadcast_multiply_fusion), kind=kOutput, calls=%fused_computation.204 | convolution fusion | flops 6446383104 | bytes 24131584 | tf_op jit(solution)/shard_map/dot_general | solution.py:281
  279.7 20.8 %fusion.42 = (f32[4096]{0:T(1024)S(1)}, bf16[768,4096]{1,0:T(8,128)(2,1)}) fusion(f32[768,4096]{1,0:T(8,128)} %fusion.35, f32[4096]{0:T(1024)S(1)} %slice_bitcast_fusion, bf16[4096,1024]{1,0:T(8,128)(2,1)} %bitcast.84, bf16[768,1024]{1,0:T(8,128)(2,1)S(1)} %copy-done.22), kind=kOutput, calls=%fused_computation.211 | convolution fusion | flops 6511652864 | bytes 28868608 | tf_op jit(solution)/shard_map/dot_general | solution.py:37
  300.4 11.9 %multiply_reduce_fusion = (f32[1024]{0:T(1024)S(1)}, f32[768]{0:T(1024)S(1)}, f32[1024]{0:T(1024)S(1)}, f32[768,1024]{1,0:T(8,128)S(1)}) fusion(f32[768,1024]{1,0:T(8,128)S(1)} %copy-done.9, f32[768]{0:T(1024)S(1)} %fusion.29, f32[768]{0:T(1024)S(1)} %broadcast_multiply_fusion, f32[1024]{0:T(1024)S(1)} %mul.190, bf16[1024,4096]{1,0:T(8,128)(2,1)} %bitcast.87, ...), kind=kOutput, calls=%fused_computation.51 | convolution fusion | flops 6448739328 | bytes 20993024 | tf_op jit(solution)/shard_map/dot_general | solution.py:37
  316.2 36.5 %shard_map.255 = (bf16[768,1024]{1,0:T(8,128)(2,1)S(1)}, bf16[768,1024]{1,0:T(8,128)(2,1)S(1)}, bf16[768,1024]{1,0:T(8,128)(2,1)S(1)}, f32[2,2,1024]{2,1,0:T(2,128)S(1)}) custom-call(bf16[768,1024]{1,0:T(8,128)(2,1)S(1)} %convolution_convert_fusion.4.g_ref, bf16[2,16,384,384]{3,2,1,0:T(8,128)(2,1)S(1)} %bitcast.77, ...), custom_call_target="tpu_custom_call" | custom-call | flops 3019898880 | bytes 20971520 | tf_op jit(solution)/shard_map/pallas_call | solution.py:198
  354.3 7.5 %fusion.37 = (f32[1024]{0:T(1024)S(1)}, f32[768]{0:T(1024)S(1)}, f32[768,1024]{1,0:T(8,128)S(1)}) fusion(f32[1024]{0:T(1024)S(1)} %mul.184, f32[768]{0:T(1024)S(1)} %broadcast_multiply_fusion.1, bf16[768,1024]{1,0:T(8,128)(2,1)S(1)} %copy-done.3, bf16[768,3072]{1,0:T(8,128)(2,1)S(1)} %constant_dynamic-update-slice_fusion, bf16[1024,3072]{1,0:T(8,128)(2,1)} %bitcast.89), kind=kOutput, calls=%fused_computation.206 | convolution fusion | flops 4836554752 | bytes 15742976 | tf_op jit(solution)/shard_map/dot_general | solution.py:37
  361.9 7.5 %convolution_convert_fusion.2 = bf16[1024,3072]{1,0:T(8,128)(2,1)} fusion(bf16[768,3072]{1,0:T(8,128)(2,1)S(1)} %constant_dynamic-update-slice_fusion, bf16[768,1024]{1,0:T(8,128)(2,1)S(1)} %copy-done.3, f32[1024]{0:T(1024)S(1)} %add.269, f32[1024]{0:T(1024)S(1)} %mul.184, f32[768]{0:T(1024)S(1)} %fusion.28, f32[768]{0:T(1024)S(1)} %broadcast_multiply_fusion.1), kind=kOutput, calls=%fused_computation.23 | convolution fusion | flops 4839702528 | bytes 12597248 | tf_op jit(solution)/shard_map/dot_general | solution.py:31
  372.6 12.1 %convolution_convert_fusion.1 = bf16[1024,4096]{1,0:T(8,128)(2,1)} fusion(bf16[768,4096]{1,0:T(8,128)(2,1)} %get-tuple-element.107, f32[768,1024]{1,0:T(8,128)S(1)} %copy-done.9, f32[1024]{0:T(1024)S(1)} %add.279, f32[1024]{0:T(1024)S(1)} %mul.190, f32[768]{0:T(1024)S(1)} %fusion.29, f32[768]{0:T(1024)S(1)} %broadcast_multiply_fusion), kind=kOutput, calls=%fused_computation.20 | convolution fusion | flops 6450577408 | bytes 17840128 | tf_op jit(solution)/shard_map/dot_general | solution.py:31
  384.8 14.7 %convolution_convert_fusion = bf16[4096,1024]{1,0:T(8,128)(2,1)} fusion(bf16[768,1024]{1,0:T(8,128)(2,1)S(1)} %copy-done.23, f32[768,4096]{1,0:T(8,128)} %fusion.35, f32[4096]{0:T(1024)S(1)} %slice_bitcast_fusion), kind=kOutput, calls=%fused_computation.19 | convolution fusion | flops 6478102528 | bytes 22560768 | tf_op jit(solution)/shard_map/dot_general | solution.py:31
  419.3 15.0 %add_convert_fusion.7 = bf16[768,1024]{1,0:T(8,128)(2,1)} fusion(f32[768,1024]{1,0:T(8,128)S(1)} %copy-done.10, bf16[4096,1024]{1,0:T(8,128)(2,1)} %bitcast.85, f32[1024]{0:T(1024)S(1)} %copy-done.30, f32[768,4096]{1,0:T(8,128)} %fusion.35, f32[4096]{0:T(1024)S(1)} %slice_bitcast_fusion), kind=kOutput, calls=%fused_computation.58 | convolution fusion | flops 6476267520 | bytes 25710592 | tf_op jit(solution)/shard_map/dot_general | solution.py:284
  439.9 8.9 %collective-permute-done.36 = bf16[2,2,2,1,1,32,1024]{6,5,4,3,2,1,0:T(8,128)(2,1)S(1)} collective-permute-done((bf16[2,2,2,1,1,32,1024]{6,5,4,3,2,1,0:T(8,128)(2,1)S(1)}, bf16[2,2,2,1,1,32,1024]{6,5,4,3,2,1,0:T(8,128)(2,1)S(1)}, u32[]{:S(2)}, u32[]{:S(2)}) %collective-permute-start.36) | collective-permute-done | bytes 524320 | tf_op jit(solution)/shard_map/ppermute | solution.py:52
  450.7 5.8 collective-permute-done.37
  473.9 31.6 %collective-permute-done.26 = bf16[2,2,1,1,2,32,3072]{6,5,4,3,2,1,0:T(8,128)(2,1)} collective-permute-done((bf16[2,2,1,1,2,32,3072]{6,5,4,3,2,1,0:T(8,128)(2,1)}, bf16[2,2,1,1,2,32,3072]{6,5,4,3,2,1,0:T(8,128)(2,1)}, u32[]{:S(2)}, u32[]{:S(2)}) %collective-permute-start.26) | collective-permute-done | bytes 1572896 | tf_op jit(solution)/shard_map/ppermute | solution.py:52
  515.7 13.5 %collective-permute-done.27 = bf16[2,2,1,1,1,32,3072]{6,5,4,3,2,1,0:T(8,128)(2,1)} collective-permute-done((bf16[2,2,1,1,1,32,3072]{6,5,4,3,2,1,0:T(8,128)(2,1)}, bf16[2,2,1,1,1,32,3072]{6,5,4,3,2,1,0:T(8,128)(2,1)}, u32[]{:S(2)}, u32[]{:S(2)}) %collective-permute-start.27) | collective-permute-done | bytes 786464 | tf_op jit(solution)/shard_map/ppermute | solution.py:52
  531.3 14.9 %collective-permute-done.41 = bf16[2,2,1,1,2,32,4096]{6,5,4,3,2,1,0:T(8,128)(2,1)S(1)} collective-permute-done((bf16[2,2,1,1,2,32,4096]{6,5,4,3,2,1,0:T(8,128)(2,1)S(1)}, bf16[2,2,1,1,2,32,4096]{6,5,4,3,2,1,0:T(8,128)(2,1)S(1)}, u32[]{:S(2)}, u32[]{:S(2)}) %collective-permute-start.41) | collective-permute-done | bytes 2097184 | tf_op jit(solution)/shard_map/ppermute | solution.py:52
  549.5 24.5 %collective-permute-done.46 = bf16[2,2,2,1,1,128,1024]{6,5,4,3,2,1,0:T(8,128)(2,1)S(1)} collective-permute-done((bf16[2,2,2,1,1,128,1024]{6,5,4,3,2,1,0:T(8,128)(2,1)S(1)}, bf16[2,2,2,1,1,128,1024]{6,5,4,3,2,1,0:T(8,128)(2,1)S(1)}, u32[]{:S(2)}, u32[]{:S(2)}) %collective-permute-start.46) | collective-permute-done | bytes 2097184 | tf_op jit(solution)/shard_map/ppermute | solution.py:52
  575.8 11.6 %collective-permute-done.42 = bf16[2,2,1,1,1,32,4096]{6,5,4,3,2,1,0:T(8,128)(2,1)S(1)} collective-permute-done((bf16[2,2,1,1,1,32,4096]{6,5,4,3,2,1,0:T(8,128)(2,1)S(1)}, bf16[2,2,1,1,1,32,4096]{6,5,4,3,2,1,0:T(8,128)(2,1)S(1)}, u32[]{:S(2)}, u32[]{:S(2)}) %collective-permute-start.42) | collective-permute-done | bytes 1048608 | tf_op jit(solution)/shard_map/ppermute | solution.py:52
  591.2 9.9 %collective-permute-done.43 = bf16[2,1,1,1,1,32,4096]{6,5,4,3,2,1,0:T(8,128)(2,1)S(1)} collective-permute-done((bf16[2,1,1,1,1,32,4096]{6,5,4,3,2,1,0:T(8,128)(2,1)S(1)}, bf16[2,1,1,1,1,32,4096]{6,5,4,3,2,1,0:T(8,128)(2,1)S(1)}, u32[]{:S(2)}, u32[]{:S(2)}) %collective-permute-start.43) | collective-permute-done | bytes 524320 | tf_op jit(solution)/shard_map/ppermute | solution.py:52
  604.5 7.7 %collective-permute-done.48 = bf16[2,1,1,1,1,128,1024]{6,5,4,3,2,1,0:T(8,128)(2,1)S(1)} collective-permute-done((bf16[2,1,1,1,1,128,1024]{6,5,4,3,2,1,0:T(8,128)(2,1)S(1)}, bf16[2,1,1,1,1,128,1024]{6,5,4,3,2,1,0:T(8,128)(2,1)S(1)}, u32[]{:S(2)}, u32[]{:S(2)}) %collective-permute-start.48) | collective-permute-done | bytes 524320 | tf_op jit(solution)/shard_map/ppermute | solution.py:52
  613.4 8.2 %collective-permute-done.49 = bf16[1,1,1,1,1,128,1024]{6,5,4,3,2,1,0:T(8,128)(2,1)S(1)} collective-permute-done((bf16[1,1,1,1,1,128,1024]{6,5,4,3,2,1,0:T(8,128)(2,1)S(1)}, bf16[1,1,1,1,1,128,1024]{6,5,4,3,2,1,0:T(8,128)(2,1)S(1)}, u32[]{:S(2)}, u32[]{:S(2)}) %collective-permute-start.49) | collective-permute-done | bytes 262176 | tf_op jit(solution)/shard_map/ppermute | solution.py:52
  (307 shorter events, 180.0 us)
Async XLA Ops:
  10.2 41.4 %collective-permute-start.5 = (bf16[1,1,1,1,1,32,3072]{6,5,4,3,2,1,0:T(8,128)(2,1)}, bf16[1,1,1,1,1,32,3072]{6,5,4,3,2,1,0:T(8,128)(2,1)S(1)}, u32[]{:S(2)}, u32[]{:S(2)}) collective-permute-start(bf16[1,1,1,1,1,32,3072]{6,5,4,3,2,1,0:T(8,128)(2,1)} %bitcast.100), channel_id=1, source_target_pairs={{0,16},{1,17},{2,18},{3,19},{4,20},{5,21},{6,22},{7,23},{8,24},{9,... | collective-permute-start | bytes 589832 | tf_op jit(solution)/shard_map/ppermute | solution.py:52
  10.3 26.8 %collective-permute-start.10 = (bf16[1,1,1,1,1,32,1024]{6,5,4,3,2,1,0:T(8,128)(2,1)}, bf16[1,1,1,1,1,32,1024]{6,5,4,3,2,1,0:T(8,128)(2,1)S(1)}, u32[]{:S(2)}, u32[]{:S(2)}) collective-permute-start(bf16[1,1,1,1,1,32,1024]{6,5,4,3,2,1,0:T(8,128)(2,1)} %bitcast.101), channel_id=1, source_target_pairs={{0,16},{1,17},{2,18},{3,19},{4,20},{5,21},{6,22},{7,23},{8,24},{9,... | collective-permute-start | bytes 196616 | tf_op jit(solution)/shard_map/ppermute | solution.py:52
  13.2 38.6 %collective-permute-start.20 = (bf16[1,1,1,1,1,128,1024]{6,5,4,3,2,1,0:T(8,128)(2,1)}, bf16[1,1,1,1,1,128,1024]{6,5,4,3,2,1,0:T(8,128)(2,1)S(1)}, u32[]{:S(2)}, u32[]{:S(2)}) collective-permute-start(bf16[1,1,1,1,1,128,1024]{6,5,4,3,2,1,0:T(8,128)(2,1)} %bitcast.98), channel_id=1, source_target_pairs={{0,16},{1,17},{2,18},{3,19},{4,20},{5,21},{6,22},{7,23},{8,24},{9,... | collective-permute-start | bytes 786440 | tf_op jit(solution)/shard_map/ppermute | solution.py:52
  13.3 40.7 %collective-permute-start.15 = (bf16[1,1,1,1,1,32,4096]{6,5,4,3,2,1,0:T(8,128)(2,1)}, bf16[1,1,1,1,1,32,4096]{6,5,4,3,2,1,0:T(8,128)(2,1)S(1)}, u32[]{:S(2)}, u32[]{:S(2)}) collective-permute-start(bf16[1,1,1,1,1,32,4096]{6,5,4,3,2,1,0:T(8,128)(2,1)} %bitcast.99), channel_id=1, source_target_pairs={{0,16},{1,17},{2,18},{3,19},{4,20},{5,21},{6,22},{7,23},{8,24},{9,... | collective-permute-start | bytes 786440 | tf_op jit(solution)/shard_map/ppermute | solution.py:52
  51.9 23.1 %collective-permute-start.21 = (bf16[2,1,1,1,1,128,1024]{6,5,4,3,2,1,0:T(8,128)(2,1)S(1)}, bf16[2,1,1,1,1,128,1024]{6,5,4,3,2,1,0:T(8,128)(2,1)S(1)}, u32[]{:S(2)}, u32[]{:S(2)}) collective-permute-start(bf16[2,1,1,1,1,128,1024]{6,5,4,3,2,1,0:T(8,128)(2,1)S(1)} %pad_maximum_fusion.16), channel_id=1, source_target_pairs={{0,8},{1,9},{2,10},{3,11},{4,12},{5,13},{6,14},{7,15},{8,0},{9,1},... | collective-permute-start | bytes 1572872 | tf_op jit(solution)/shard_map/ppermute | solution.py:52
  54.1 31.0 %collective-permute-start.16 = (bf16[2,1,1,1,1,32,4096]{6,5,4,3,2,1,0:T(8,128)(2,1)S(1)}, bf16[2,1,1,1,1,32,4096]{6,5,4,3,2,1,0:T(8,128)(2,1)S(1)}, u32[]{:S(2)}, u32[]{:S(2)}) collective-permute-start(bf16[2,1,1,1,1,32,4096]{6,5,4,3,2,1,0:T(8,128)(2,1)S(1)} %pad_maximum_fusion.15), channel_id=1, source_target_pairs={{0,8},{1,9},{2,10},{3,11},{4,12},{5,13},{6,14},{7,15},{8,0},{9,1},... | collective-permute-start | bytes 1572872 | tf_op jit(solution)/shard_map/ppermute | solution.py:52
  58.5 28.3 %collective-permute-start.13 = (bf16[2,2,1,1,2,32,1024]{6,5,4,3,2,1,0:T(8,128)(2,1)S(1)}, bf16[2,2,1,1,2,32,1024]{6,5,4,3,2,1,0:T(8,128)(2,1)S(1)}, u32[]{:S(2)}, u32[]{:S(2)}) collective-permute-start(bf16[2,2,1,1,2,32,1024]{6,5,4,3,2,1,0:T(8,128)(2,1)S(1)} %pad_maximum_fusion.14), channel_id=1, source_target_pairs={{0,4},{1,5},{2,6},{3,7},{4,0},{5,1},{6,2},{7,3},{8,12},{9,13},{10,... | collective-permute-start | bytes 1572872 | tf_op jit(solution)/shard_map/ppermute | solution.py:52
  63.9 26.2 %collective-permute-start.7 = (bf16[2,2,1,1,1,32,3072]{6,5,4,3,2,1,0:T(8,128)(2,1)S(1)}, bf16[2,2,1,1,1,32,3072]{6,5,4,3,2,1,0:T(8,128)(2,1)S(1)}, u32[]{:S(2)}, u32[]{:S(2)}) collective-permute-start(bf16[2,2,1,1,1,32,3072]{6,5,4,3,2,1,0:T(8,128)(2,1)S(1)} %pad_maximum_fusion.13), channel_id=1, source_target_pairs={{0,4},{1,5},{2,6},{3,7},{4,0},{5,1},{6,2},{7,3},{8,12},{9,13},{10,... | collective-permute-start | bytes 2359304 | tf_op jit(solution)/shard_map/ppermute | solution.py:52
  75.2 26.2 %collective-permute-start.22 = (bf16[2,2,1,1,1,128,1024]{6,5,4,3,2,1,0:T(8,128)(2,1)S(1)}, bf16[2,2,1,1,1,128,1024]{6,5,4,3,2,1,0:T(8,128)(2,1)S(1)}, u32[]{:S(2)}, u32[]{:S(2)}) collective-permute-start(bf16[2,2,1,1,1,128,1024]{6,5,4,3,2,1,0:T(8,128)(2,1)S(1)} %pad_maximum_fusion.12), channel_id=1, source_target_pairs={{0,1},{1,0},{2,3},{3,2},{4,5},{5,4},{6,7},{7,6},{8,9},{9,8},{10,11... | collective-permute-start | bytes 3145736 | tf_op jit(solution)/shard_map/ppermute | solution.py:52
  85.3 27.3 %collective-permute-start.17 = (bf16[2,2,1,1,1,32,4096]{6,5,4,3,2,1,0:T(8,128)(2,1)S(1)}, bf16[2,2,1,1,1,32,4096]{6,5,4,3,2,1,0:T(8,128)(2,1)S(1)}, u32[]{:S(2)}, u32[]{:S(2)}) collective-permute-start(bf16[2,2,1,1,1,32,4096]{6,5,4,3,2,1,0:T(8,128)(2,1)S(1)} %pad_maximum_fusion.11), channel_id=1, source_target_pairs={{0,4},{1,5},{2,6},{3,7},{4,0},{5,1},{6,2},{7,3},{8,12},{9,13},{10,... | collective-permute-start | bytes 3145736 | tf_op jit(solution)/shard_map/ppermute | solution.py:52
  88.1 50.5 %collective-permute-start.14 = (bf16[2,2,2,1,2,32,1024]{6,5,4,3,2,1,0:T(8,128)(2,1)}, bf16[2,2,2,1,2,32,1024]{6,5,4,3,2,1,0:T(8,128)(2,1)}, u32[]{:S(2)}, u32[]{:S(2)}) collective-permute-start(bf16[2,2,2,1,2,32,1024]{6,5,4,3,2,1,0:T(8,128)(2,1)} %pad_maximum_fusion.10), channel_id=1, source_target_pairs={{0,2},{1,3},{2,0},{3,1},{4,6},{5,7},{6,4},{7,5},{8,10},{9,11},{10,... | collective-permute-start | bytes 3145736 | tf_op jit(solution)/shard_map/ppermute | solution.py:52
  90.4 44.7 %collective-permute-start.8 = (bf16[2,2,2,1,1,32,3072]{6,5,4,3,2,1,0:T(8,128)(2,1)S(1)}, bf16[2,2,2,1,1,32,3072]{6,5,4,3,2,1,0:T(8,128)(2,1)S(1)}, u32[]{:S(2)}, u32[]{:S(2)}) collective-permute-start(bf16[2,2,2,1,1,32,3072]{6,5,4,3,2,1,0:T(8,128)(2,1)S(1)} %pad_maximum_fusion.9), channel_id=1, source_target_pairs={{0,1},{1,0},{2,3},{3,2},{4,5},{5,4},{6,7},{7,6},{8,9},{9,8},{10,11... | collective-permute-start | bytes 4718600 | tf_op jit(solution)/shard_map/ppermute | solution.py:52
  103.2 52.8 %collective-permute-start.23 = (bf16[2,2,1,1,2,128,1024]{6,5,4,3,2,1,0:T(8,128)(2,1)}, bf16[2,2,1,1,2,128,1024]{6,5,4,3,2,1,0:T(8,128)(2,1)}, u32[]{:S(2)}, u32[]{:S(2)}) collective-permute-start(bf16[2,2,1,1,2,128,1024]{6,5,4,3,2,1,0:T(8,128)(2,1)} %pad_maximum_fusion.8), channel_id=1, source_target_pairs={{0,4},{1,5},{2,6},{3,7},{4,0},{5,1},{6,2},{7,3},{8,12},{9,13},{10,... | collective-permute-start | bytes 6291464 | tf_op jit(solution)/shard_map/ppermute | solution.py:52
  114.4 62.4 %collective-permute-start.18 = (bf16[2,2,2,1,1,32,4096]{6,5,4,3,2,1,0:T(8,128)(2,1)}, bf16[2,2,2,1,1,32,4096]{6,5,4,3,2,1,0:T(8,128)(2,1)}, u32[]{:S(2)}, u32[]{:S(2)}) collective-permute-start(bf16[2,2,2,1,1,32,4096]{6,5,4,3,2,1,0:T(8,128)(2,1)} %pad_maximum_fusion.7), channel_id=1, source_target_pairs={{0,1},{1,0},{2,3},{3,2},{4,5},{5,4},{6,7},{7,6},{8,9},{9,8},{10,11... | collective-permute-start | bytes 6291464 | tf_op jit(solution)/shard_map/ppermute | solution.py:52
  137.5 43.7 %collective-permute-start.9 = (bf16[2,2,2,1,2,32,3072]{6,5,4,3,2,1,0:T(8,128)(2,1)}, bf16[2,2,2,1,2,32,3072]{6,5,4,3,2,1,0:T(8,128)(2,1)}, u32[]{:S(2)}, u32[]{:S(2)}) collective-permute-start(bf16[2,2,2,1,2,32,3072]{6,5,4,3,2,1,0:T(8,128)(2,1)} %pad_maximum_fusion.5), channel_id=1, source_target_pairs={{0,2},{1,3},{2,0},{3,1},{4,6},{5,7},{6,4},{7,5},{8,10},{9,11},{10,... | collective-permute-start | bytes 9437192 | tf_op jit(solution)/shard_map/ppermute | solution.py:52
  160.3 79.2 %collective-permute-start.24 = (bf16[2,2,2,1,2,128,1024]{6,5,4,3,2,1,0:T(8,128)(2,1)}, bf16[2,2,2,1,2,128,1024]{6,5,4,3,2,1,0:T(8,128)(2,1)}, u32[]{:S(2)}, u32[]{:S(2)}) collective-permute-start(bf16[2,2,2,1,2,128,1024]{6,5,4,3,2,1,0:T(8,128)(2,1)} %pad_maximum_fusion.4), channel_id=1, source_target_pairs={{0,2},{1,3},{2,0},{3,1},{4,6},{5,7},{6,4},{7,5},{8,10},{9,11},{10,... | collective-permute-start | bytes 12582920 | tf_op jit(solution)/shard_map/ppermute | solution.py:52
  181.1 71.6 %collective-permute-start.19 = (bf16[2,2,2,1,2,32,4096]{6,5,4,3,2,1,0:T(8,128)(2,1)}, bf16[2,2,2,1,2,32,4096]{6,5,4,3,2,1,0:T(8,128)(2,1)}, u32[]{:S(2)}, u32[]{:S(2)}) collective-permute-start(bf16[2,2,2,1,2,32,4096]{6,5,4,3,2,1,0:T(8,128)(2,1)} %pad_maximum_fusion.3), channel_id=1, source_target_pairs={{0,2},{1,3},{2,0},{3,1},{4,6},{5,7},{6,4},{7,5},{8,10},{9,11},{10,... | collective-permute-start | bytes 12582920 | tf_op jit(solution)/shard_map/ppermute | solution.py:52
  407.7 55.8 %collective-permute-start.25 = (bf16[2,2,2,1,2,32,3072]{6,5,4,3,2,1,0:T(8,128)(2,1)S(1)}, bf16[2,2,2,1,2,32,3072]{6,5,4,3,2,1,0:T(8,128)(2,1)}, u32[]{:S(2)}, u32[]{:S(2)}) collective-permute-start(bf16[2,2,2,1,2,32,3072]{6,5,4,3,2,1,0:T(8,128)(2,1)S(1)} %constant_dynamic-slice_fusion.28), channel_id=1, source_target_pairs={{0,2},{1,3},{2,0},{3,1},{4,6},{5,7},{6,4},{7,5},{8,10},{9,11},{10,... | collective-permute-start | bytes 9437192 | tf_op jit(solution)/shard_map/ppermute | solution.py:52
  409.0 25.4 %collective-permute-start.35 = (bf16[2,2,2,1,2,32,1024]{6,5,4,3,2,1,0:T(8,128)(2,1)S(1)}, bf16[2,2,2,1,2,32,1024]{6,5,4,3,2,1,0:T(8,128)(2,1)S(1)}, u32[]{:S(2)}, u32[]{:S(2)}) collective-permute-start(bf16[2,2,2,1,2,32,1024]{6,5,4,3,2,1,0:T(8,128)(2,1)S(1)} %constant_dynamic-slice_fusion.14), channel_id=1, source_target_pairs={{0,2},{1,3},{2,0},{3,1},{4,6},{5,7},{6,4},{7,5},{8,10},{9,11},{10,... | collective-permute-start | bytes 3145736 | tf_op jit(solution)/shard_map/ppermute | solution.py:52
  418.6 49.8 %collective-permute-start.40 = (bf16[2,2,2,1,2,32,4096]{6,5,4,3,2,1,0:T(8,128)(2,1)}, bf16[2,2,2,1,2,32,4096]{6,5,4,3,2,1,0:T(8,128)(2,1)S(1)}, u32[]{:S(2)}, u32[]{:S(2)}) collective-permute-start(bf16[2,2,2,1,2,32,4096]{6,5,4,3,2,1,0:T(8,128)(2,1)} %constant_dynamic-slice_fusion.9), channel_id=1, source_target_pairs={{0,2},{1,3},{2,0},{3,1},{4,6},{5,7},{6,4},{7,5},{8,10},{9,11},{10,... | collective-permute-start | bytes 12582920 | tf_op jit(solution)/shard_map/ppermute | solution.py:52
  418.6 15.7 %collective-permute-start.33 = (f32[2,1,1,1,1,1,384]{6,5,4,3,2,1,0:T(1,128)S(1)}, f32[2,1,1,1,1,1,384]{6,5,4,3,2,1,0:T(1,128)S(1)}, u32[]{:S(2)}, u32[]{:S(2)}) collective-permute-start(f32[2,1,1,1,1,1,384]{6,5,4,3,2,1,0:T(1,128)S(1)} %constant_dynamic-slice_fusion.17), channel_id=1, source_target_pairs={{0,8},{1,9},{2,10},{3,11},{4,12},{5,13},{6,14},{7,15},{8,0},{9,1},... | collective-permute-start | bytes 9224 | tf_op jit(solution)/shard_map/ppermute | solution.py:52
  439.6 70.0 %collective-permute-start.45 = (bf16[2,2,2,1,2,128,1024]{6,5,4,3,2,1,0:T(8,128)(2,1)}, bf16[2,2,2,1,2,128,1024]{6,5,4,3,2,1,0:T(8,128)(2,1)}, u32[]{:S(2)}, u32[]{:S(2)}) collective-permute-start(bf16[2,2,2,1,2,128,1024]{6,5,4,3,2,1,0:T(8,128)(2,1)} %constant_dynamic-slice_fusion.4), channel_id=1, source_target_pairs={{0,2},{1,3},{2,0},{3,1},{4,6},{5,7},{6,4},{7,5},{8,10},{9,11},{10,... | collective-permute-start | bytes 12582920 | tf_op jit(solution)/shard_map/ppermute | solution.py:52
  461.8 47.3 %collective-permute-start.39 = (bf16[1,1,1,1,1,32,1024]{6,5,4,3,2,1,0:T(8,128)(2,1)S(1)}, bf16[1,1,1,1,1,32,1024]{6,5,4,3,2,1,0:T(8,128)(2,1)S(1)}, u32[]{:S(2)}, u32[]{:S(2)}) collective-permute-start(bf16[1,1,1,1,1,32,1024]{6,5,4,3,2,1,0:T(8,128)(2,1)S(1)} %constant_dynamic-slice_fusion.10), channel_id=1, source_target_pairs={{0,16},{1,17},{2,18},{3,19},{4,20},{5,21},{6,22},{7,23},{8,24},{9,... | collective-permute-start | bytes 196616 | tf_op jit(solution)/shard_map/ppermute | solution.py:52
  467.8 37.6 %collective-permute-start.26 = (bf16[2,2,1,1,2,32,3072]{6,5,4,3,2,1,0:T(8,128)(2,1)}, bf16[2,2,1,1,2,32,3072]{6,5,4,3,2,1,0:T(8,128)(2,1)}, u32[]{:S(2)}, u32[]{:S(2)}) collective-permute-start(bf16[2,2,1,1,2,32,3072]{6,5,4,3,2,1,0:T(8,128)(2,1)} %constant_dynamic-slice_fusion.27), channel_id=1, source_target_pairs={{0,4},{1,5},{2,6},{3,7},{4,0},{5,1},{6,2},{7,3},{8,12},{9,13},{10,... | collective-permute-start | bytes 4718600 | tf_op jit(solution)/shard_map/ppermute | solution.py:52
  472.3 73.9 %collective-permute-start.41 = (bf16[2,2,1,1,2,32,4096]{6,5,4,3,2,1,0:T(8,128)(2,1)S(1)}, bf16[2,2,1,1,2,32,4096]{6,5,4,3,2,1,0:T(8,128)(2,1)S(1)}, u32[]{:S(2)}, u32[]{:S(2)}) collective-permute-start(bf16[2,2,1,1,2,32,4096]{6,5,4,3,2,1,0:T(8,128)(2,1)S(1)} %constant_dynamic-slice_fusion.8), channel_id=1, source_target_pairs={{0,4},{1,5},{2,6},{3,7},{4,0},{5,1},{6,2},{7,3},{8,12},{9,13},{10,... | collective-permute-start | bytes 6291464 | tf_op jit(solution)/shard_map/ppermute | solution.py:52
  508.4 20.8 %collective-permute-start.27 = (bf16[2,2,1,1,1,32,3072]{6,5,4,3,2,1,0:T(8,128)(2,1)}, bf16[2,2,1,1,1,32,3072]{6,5,4,3,2,1,0:T(8,128)(2,1)}, u32[]{:S(2)}, u32[]{:S(2)}) collective-permute-start(bf16[2,2,1,1,1,32,3072]{6,5,4,3,2,1,0:T(8,128)(2,1)} %constant_dynamic-slice_fusion.26), channel_id=1, source_target_pairs={{0,1},{1,0},{2,3},{3,2},{4,5},{5,4},{6,7},{7,6},{8,9},{9,8},{10,11... | collective-permute-start | bytes 2359304 | tf_op jit(solution)/shard_map/ppermute | solution.py:52
  514.2 59.9 %collective-permute-start.46 = (bf16[2,2,2,1,1,128,1024]{6,5,4,3,2,1,0:T(8,128)(2,1)S(1)}, bf16[2,2,2,1,1,128,1024]{6,5,4,3,2,1,0:T(8,128)(2,1)S(1)}, u32[]{:S(2)}, u32[]{:S(2)}) collective-permute-start(bf16[2,2,2,1,1,128,1024]{6,5,4,3,2,1,0:T(8,128)(2,1)S(1)} %constant_dynamic-slice_fusion.3), channel_id=1, source_target_pairs={{0,1},{1,0},{2,3},{3,2},{4,5},{5,4},{6,7},{7,6},{8,9},{9,8},{10,11... | collective-permute-start | bytes 6291464 | tf_op jit(solution)/shard_map/ppermute | solution.py:52
  530.6 17.4 %collective-permute-start.28 = (bf16[2,1,1,1,1,32,3072]{6,5,4,3,2,1,0:T(8,128)(2,1)S(1)}, bf16[2,1,1,1,1,32,3072]{6,5,4,3,2,1,0:T(8,128)(2,1)S(1)}, u32[]{:S(2)}, u32[]{:S(2)}) collective-permute-start(bf16[2,1,1,1,1,32,3072]{6,5,4,3,2,1,0:T(8,128)(2,1)S(1)} %constant_dynamic-slice_fusion.25), channel_id=1, source_target_pairs={{0,8},{1,9},{2,10},{3,11},{4,12},{5,13},{6,14},{7,15},{8,0},{9,1},... | collective-permute-start | bytes 1179656 | tf_op jit(solution)/shard_map/ppermute | solution.py:52
  547.3 40.1 %collective-permute-start.42 = (bf16[2,2,1,1,1,32,4096]{6,5,4,3,2,1,0:T(8,128)(2,1)S(1)}, bf16[2,2,1,1,1,32,4096]{6,5,4,3,2,1,0:T(8,128)(2,1)S(1)}, u32[]{:S(2)}, u32[]{:S(2)}) collective-permute-start(bf16[2,2,1,1,1,32,4096]{6,5,4,3,2,1,0:T(8,128)(2,1)S(1)} %constant_dynamic-slice_fusion.7), channel_id=1, source_target_pairs={{0,1},{1,0},{2,3},{3,2},{4,5},{5,4},{6,7},{7,6},{8,9},{9,8},{10,11... | collective-permute-start | bytes 3145736 | tf_op jit(solution)/shard_map/ppermute | solution.py:52
  548.1 40.3 %collective-permute-start.29 = (bf16[1,1,1,1,1,32,3072]{6,5,4,3,2,1,0:T(8,128)(2,1)S(1)}, bf16[1,1,1,1,1,32,3072]{6,5,4,3,2,1,0:T(8,128)(2,1)S(1)}, u32[]{:S(2)}, u32[]{:S(2)}) collective-permute-start(bf16[1,1,1,1,1,32,3072]{6,5,4,3,2,1,0:T(8,128)(2,1)S(1)} %constant_dynamic-slice_fusion.24), channel_id=1, source_target_pairs={{0,16},{1,17},{2,18},{3,19},{4,20},{5,21},{6,22},{7,23},{8,24},{9,... | collective-permute-start | bytes 589832 | tf_op jit(solution)/shard_map/ppermute | solution.py:52
  575.2 14.9 %collective-permute-start.47 = (bf16[2,2,1,1,1,128,1024]{6,5,4,3,2,1,0:T(8,128)(2,1)S(1)}, bf16[2,2,1,1,1,128,1024]{6,5,4,3,2,1,0:T(8,128)(2,1)S(1)}, u32[]{:S(2)}, u32[]{:S(2)}) collective-permute-start(bf16[2,2,1,1,1,128,1024]{6,5,4,3,2,1,0:T(8,128)(2,1)S(1)} %constant_dynamic-slice_fusion.2), channel_id=1, source_target_pairs={{0,4},{1,5},{2,6},{3,7},{4,0},{5,1},{6,2},{7,3},{8,12},{9,13},{10,... | collective-permute-start | bytes 3145736 | tf_op jit(solution)/shard_map/ppermute | solution.py:52
  590.5 21.7 %collective-permute-start.48 = (bf16[2,1,1,1,1,128,1024]{6,5,4,3,2,1,0:T(8,128)(2,1)S(1)}, bf16[2,1,1,1,1,128,1024]{6,5,4,3,2,1,0:T(8,128)(2,1)S(1)}, u32[]{:S(2)}, u32[]{:S(2)}) collective-permute-start(bf16[2,1,1,1,1,128,1024]{6,5,4,3,2,1,0:T(8,128)(2,1)S(1)} %constant_dynamic-slice_fusion.1), channel_id=1, source_target_pairs={{0,8},{1,9},{2,10},{3,11},{4,12},{5,13},{6,14},{7,15},{8,0},{9,1},... | collective-permute-start | bytes 1572872 | tf_op jit(solution)/shard_map/ppermute | solution.py:52
  (56 other events, 624.9 us)

commit v2 on v1

--- a/solution.py
+++ b/solution.py
@@ -52,36 +52,62 @@
     return lax.ppermute(piece, AXES, [(i, i ^ (1 << bit)) for i in range(count)])
 
 
-def gather(shard, order):
+def after(value, *others):
+    return lax.optimization_barrier((value,) + others)[0]
+
+
+def gather(shard, order, wait_for=None):
     count = lax.axis_size("dp") * lax.axis_size("fsdp")
     bits = (count - 1).bit_length()
     index = lax.axis_index(AXES)
     held = shard.reshape((1,) * bits + shard.shape)
-    for bit in order:
+    if wait_for is not None:
+        held = after(held, wait_for)
+    mark = held
+    for step, bit in enumerate(order):
         axis = bits - 1 - bit
         got = swap(held, bit, count)
-        upper = ((index >> bit) & 1) == 1
-        held = jnp.concatenate(
-            [jnp.where(upper, got, held), jnp.where(upper, held, got)], axis=axis
-        )
-    return held.reshape((count * shard.shape[0],) + shard.shape[1:])
-
-
-def scatter_sum(whole, order, link_type):
-    count = lax.axis_size("dp") * lax.axis_size("fsdp")
-    bits = (count - 1).bit_length()
-    index = lax.axis_index(AXES)
-    held = whole.reshape((2,) * bits + (whole.shape[0] // count,) + whole.shape[1:])
-    for step, bit in enumerate(order):
-        axis = bits - 1 - bit
-        mine = (index >> bit) & 1
-        kept = lax.dynamic_slice_in_dim(held, mine, 1, axis)
-        given = lax.dynamic_slice_in_dim(held, 1 - mine, 1, axis)
-        got = swap(given.astype(link_type), bit, count)
-        held = kept.astype(jnp.float32) + got.astype(jnp.float32)
-        if step + 1 < len(order):
-            held = held.astype(link_type)
-    return held.reshape((whole.shape[0] // count,) + whole.shape[1:])
+        side = jnp.arange(2).reshape((2,) + (1,) * (held.ndim - 1 - axis))
+        held = jnp.where(side == (index >> bit) & 1, held, got)
+        if step == len(order) - 4:
+            mark = held
+    return held.reshape((count * shard.shape[0],) + shard.shape[1:]), mark
+
+
+class Sum:
+    def __init__(self, whole, order, link_type):
+        self.count = lax.axis_size("dp") * lax.axis_size("fsdp")
+        self.bits = (self.count - 1).bit_length()
+        self.index = lax.axis_index(AXES)
+        self.shape = (whole.shape[0] // self.count,) + whole.shape[1:]
+        self.held = whole.reshape((2,) * self.bits + self.shape)
+        self.order, self.type = list(order), link_type
+
+    def give(self):
+        bit = self.order.pop(0)
+        axis = self.bits - 1 - bit
+        mine = (self.index >> bit) & 1
+        self.kept = lax.dynamic_slice_in_dim(self.held, mine, 1, axis)
+        given = lax.dynamic_slice_in_dim(self.held, 1 - mine, 1, axis)
+        given = lax.optimization_barrier(given.astype(self.type))
+        self.got = swap(given, bit, self.count)
+        return given
+
+    def take(self, *others):
+        got = after(self.got, *others) if others else self.got
+        self.held = self.kept.astype(jnp.float32) + got.astype(jnp.float32)
+        if self.order:
+            self.held = self.held.astype(self.type)
+
+    def step(self, *others):
+        self.take(*others)
+        return self.give()
+
+    def finish(self):
+        while self.order:
+            self.step()
+        self.take()
+        return self.held.reshape(self.shape)
 
 
 def distances(lengths_ref, buffer, rows):
@@ -95,7 +121,7 @@
     return jnp.where(seen, (col - row).astype(jnp.float32), far_away)
 
 
-def attend_kernel(lengths_ref, slopes_ref, q_ref, k_ref, v_ref, out_ref, probs_ref, far_ref):
+def attend_kernel(lengths_ref, slopes_ref, q_ref, k_ref, v_ref, out_ref, probs_ref, far_ref, *, first_head):
     rows, width = q_ref.shape
     buffer, pair = pl.program_id(0), pl.program_id(1)
 
@@ -114,7 +140,7 @@
         for head in range(2):
             picked = jnp.where(low_half == (head == 0), q, jnp.zeros_like(q))
             scores = against(picked, k_ref[:stop, :])
-            scores = scores + slopes_ref[2 * pair + head] * far_ref[start:stop, :stop]
+            scores = scores + slopes_ref[first_head + 2 * pair + head] * far_ref[start:stop, :stop]
             peak = jnp.max(scores, axis=-1, keepdims=True)
             exponent = jnp.exp(scores - peak)
             total = jnp.sum(exponent, axis=-1, keepdims=True)
@@ -126,15 +152,15 @@
         out_ref[start:stop, :] = jnp.where(low_half, results[0], results[1]).astype(jnp.bfloat16)
 
 
-def attend(projected, lengths, slopes):
+def attend(projected, lengths, slopes, first_head):
     rows, buffers = projected.shape[0], lengths.shape[0]
     block, width = rows // buffers, projected.shape[1] // 3
-    pairs = HEADS // 2
+    pairs = HEADS // 4
     pair_width = width // pairs
     spec = lambda part: pl.BlockSpec((block, pair_width), lambda b, p: (b, part * pairs + p))
     smem = pl.BlockSpec(memory_space=pltpu.SMEM)
     return pl.pallas_call(
-        attend_kernel,
+        functools.partial(attend_kernel, first_head=first_head),
         grid=(buffers, pairs),
         in_specs=[smem, smem, spec(0), spec(1), spec(2)],
         out_specs=[
@@ -143,7 +169,7 @@
         ],
         out_shape=[
             jax.ShapeDtypeStruct((rows, width), jnp.bfloat16),
-            jax.ShapeDtypeStruct((buffers, HEADS, block, block), jnp.bfloat16),
+            jax.ShapeDtypeStruct((buffers, HEADS // 2, block, block), jnp.bfloat16),
         ],
         scratch_shapes=[pltpu.VMEM((block, block), jnp.float32)],
         compiler_params=pltpu.CompilerParams(vmem_limit_bytes=32 * 2**20),
@@ -191,7 +217,7 @@
 def attend_back(grad_attended, probs, projected):
     rows, buffers = projected.shape[0], probs.shape[0]
     block, width = rows // buffers, projected.shape[1] // 3
-    pairs = HEADS // 2
+    pairs = HEADS // 4
     pair_width = width // pairs
     spec = lambda part: pl.BlockSpec((block, pair_width), lambda b, p: (b, part * pairs + p))
     flat = jax.ShapeDtypeStruct((rows, width), jnp.bfloat16)
@@ -238,6 +264,7 @@
     norm2_shift,
 ):
     width = tokens.shape[1]
+    half = width // 2
     inner, core, outer, bits = device_bits()
     outer_down = outer[::-1]
     gather_a = outer_down + inner[::-1] + [core]
@@ -257,64 +284,98 @@
     )
     sizes = [part.shape[0] for part in small]
     offsets = [sum(sizes[:i]) for i in range(len(sizes))]
-    packed = gather(jnp.concatenate(small).reshape(1, -1), gather_b).astype(jnp.float32)
+
+    def halves(array):
+        parts = [array[..., i * half : (i + 1) * half] for i in range(array.shape[-1] // half)]
+        return jnp.concatenate(parts[::2], axis=-1), jnp.concatenate(parts[1::2], axis=-1)
+
+    qkv_first, qkv_second = halves(qkv_weight)
+    packed, _ = gather(jnp.concatenate(small).reshape(1, -1), gather_b)
+    packed = packed.astype(jnp.float32)
     b_qv, b_dense, b_up, b_down, gain_one, shift_one, gain_two, shift_two = [
         packed[:, at : at + size].reshape(-1) for at, size in zip(offsets, sizes)
     ]
-    w_qkv = gather(qkv_weight, gather_a)
-    w_dense = gather(dense_weight, gather_b)
-    w_up = gather(up_weight, gather_a)
-    w_down = gather(down_weight, gather_b)
+    w_first, mark_first = gather(qkv_first, gather_a)
+    w_second, mark_second = gather(
+        jnp.concatenate([qkv_second, dense_weight], axis=1), gather_b
+    )
+    w_up, _ = gather(up_weight, gather_a, mark_first)
+    w_down, _ = gather(down_weight, gather_b, mark_second)
+    w_second, w_dense = w_second[:, : 3 * half], w_second[:, 3 * half :]
 
     slopes = jnp.exp2(-8.0 * jnp.arange(1, HEADS + 1, dtype=jnp.float32) / HEADS)
     inputs = tokens.astype(jnp.float32)
     bias_full = jnp.concatenate([b_qv[:width], jnp.zeros((width,), jnp.float32), b_qv[width:]])
+    bias_halves = halves(bias_full)
     normed_one = normalize(inputs, gain_one, shift_one).astype(jnp.bfloat16)
-    projected = (
-        jnp.dot(normed_one, w_qkv, preferred_element_type=jnp.float32) + bias_full
-    ).astype(jnp.bfloat16)
-    attended, probs = attend(projected, lengths, slopes)
+    projected, attended, probs = [], [], []
+    for part, weight in enumerate((w_first, w_second)):
+        projected.append(
+            (
+                jnp.dot(normed_one, weight, preferred_element_type=jnp.float32)
+                + bias_halves[part]
+            ).astype(jnp.bfloat16)
+        )
+        out, kept = attend(projected[part], lengths, slopes, part * HEADS // 2)
+        attended.append(out)
+        probs.append(kept)
+    attended = jnp.concatenate(attended, axis=1)
     residual_mid = inputs + (
         jnp.dot(attended, w_dense, preferred_element_type=jnp.float32) + b_dense
     )
     normed_two = normalize(residual_mid, gain_two, shift_two).astype(jnp.bfloat16)
     upper_pre = jnp.dot(normed_two, w_up, preferred_element_type=jnp.float32) + b_up
     activated = gelu_tanh(upper_pre).astype(jnp.bfloat16)
-    layer_out = residual_mid + (
-        jnp.dot(activated, w_down, preferred_element_type=jnp.float32) + b_down
-    )
-    mixed = layer_out.astype(jnp.bfloat16)
 
     grad_float = cotangent.astype(jnp.float32)
-    grad_down_weight = scatter_sum(
-        across(activated, cotangent).astype(jnp.bfloat16), scatter_a, jnp.bfloat16
-    )
+    down_sum = Sum(across(activated, cotangent).astype(jnp.bfloat16), scatter_a, jnp.bfloat16)
+    sent = down_sum.give()
     grad_down_bias = jnp.sum(grad_float, axis=0)
-    grad_activated = against(cotangent, w_down)
+    grad_activated = against(after(cotangent, sent), w_down)
     grad_upper = jax.vjp(gelu_tanh, upper_pre)[1](grad_activated)[0]
     grad_up_bias = jnp.sum(grad_upper, axis=0)
     grad_upper_low = grad_upper.astype(jnp.bfloat16)
-    grad_up_weight = scatter_sum(
-        across(normed_two, grad_upper_low).astype(jnp.bfloat16), scatter_b, jnp.bfloat16
-    )
-    grad_normed_two = against(grad_upper_low, w_up)
+    sent = down_sum.step(grad_upper_low)
+    up_sum = Sum(
+        across(after(normed_two, sent), grad_upper_low).astype(jnp.bfloat16),
+        scatter_b,
+        jnp.bfloat16,
+    )
+    sent = up_sum.give()
+    grad_normed_two = against(after(grad_upper_low, sent), w_up)
     grad_mid_part, grad_gain_two, grad_shift_two = jax.vjp(
         normalize, residual_mid, gain_two, shift_two
     )[1](grad_normed_two)
     grad_mid = grad_float + grad_mid_part
     grad_dense_bias = jnp.sum(grad_mid, axis=0)
     grad_mid_low = grad_mid.astype(jnp.bfloat16)
-    grad_dense_weight = scatter_sum(
-        across(attended, grad_mid_low).astype(jnp.bfloat16), scatter_a, jnp.bfloat16
-    )
-    grad_attended = against(grad_mid_low, w_dense).astype(jnp.bfloat16)
-    grad_q, grad_k, grad_v, bias_sums = attend_back(grad_attended, probs, projected)
-    grad_qv_bias = jnp.sum(bias_sums, axis=0).reshape(-1)
-    grad_projected_low = jnp.concatenate([grad_q, grad_k, grad_v], axis=1)
-    grad_qkv_weight = scatter_sum(
-        across(normed_one, grad_projected_low).astype(jnp.bfloat16), scatter_b, jnp.bfloat16
-    )
-    grad_normed_one = against(grad_projected_low, w_qkv)
+    sent = up_sum.step(grad_mid_low)
+    dense_grad = across(attended, after(grad_mid_low, sent)).astype(jnp.bfloat16)
+    grad_attended = against(after(grad_mid_low, sent, dense_grad), w_dense).astype(jnp.bfloat16)
+    first_back = attend_back(grad_attended[:, :half], probs[0], projected[0])
+    first_low = jnp.concatenate(first_back[:3], axis=1)
+    sent = down_sum.step(first_low)
+    first_grad = across(after(normed_one, sent), first_low).astype(jnp.bfloat16)
+    first_sum = Sum(
+        jnp.concatenate([first_grad, dense_grad], axis=1), scatter_a, jnp.bfloat16
+    )
+    sent = first_sum.give()
+    second_back = attend_back(after(grad_attended[:, half:], sent), probs[1], projected[1])
+    second_low = jnp.concatenate(second_back[:3], axis=1)
+    sent = (up_sum.step(second_low), down_sum.step(second_low))
+    second_sum = Sum(
+        across(after(normed_one, *sent), second_low).astype(jnp.bfloat16),
+        scatter_b,
+        jnp.bfloat16,
+    )
+    sent = (second_sum.give(),)
+    bias_sums = [jnp.sum(back[3], axis=0) for back in (first_back, second_back)]
+    grad_qv_bias = jnp.concatenate(
+        [bias_sums[0][0], bias_sums[1][0], bias_sums[0][1], bias_sums[1][1]]
+    )
+    grad_normed_first = against(after(first_low, *sent), w_first)
+    sent = (second_sum.step(grad_normed_first), first_sum.step(grad_normed_first))
+    grad_normed_one = grad_normed_first + against(after(second_low, *sent), w_second)
     grad_in_part, grad_gain_one, grad_shift_one = jax.vjp(
         normalize, inputs, gain_one, shift_one
     )[1](grad_normed_one)
@@ -330,11 +391,35 @@
         grad_gain_two,
         grad_shift_two,
     )
-    summed = scatter_sum(
+    small_sum = Sum(
         jnp.concatenate([part.reshape(count, -1) for part in small_grads], axis=1),
         scatter_a,
         jnp.float32,
-    ).reshape(-1)
+    )
+    sent = (
+        small_sum.give(),
+        second_sum.step(input_grad),
+        up_sum.step(input_grad),
+        down_sum.step(input_grad),
+    )
+    layer_out = residual_mid + (
+        jnp.dot(after(activated, *sent), w_down, preferred_element_type=jnp.float32) + b_down
+    )
+    mixed = layer_out.astype(jnp.bfloat16)
+    sent = (second_sum.step(mixed), first_sum.step(mixed), small_sum.step(mixed))
+
+    grad_down_weight, grad_up_weight = down_sum.finish(), up_sum.finish()
+    first_grad, second_grad = first_sum.finish(), second_sum.finish()
+    summed = small_sum.finish().reshape(-1)
+    grad_dense_weight = first_grad[:, 3 * half :]
+    grad_qkv_weight = jnp.concatenate(
+        [
+            grad[:, i * half : (i + 1) * half]
+            for i in range(3)
+            for grad in (first_grad, second_grad)
+        ],
+        axis=1,
+    )
     (g_qv, g_dense, g_up, g_down, g_gain_one, g_shift_one, g_gain_two, g_shift_two) = [
         summed[at : at + size] for at, size in zip(offsets, sizes)
     ]

time: 630 us -> 513 us (0.81)
  waiting for transfers between devices: 261 us -> 136 us
  local copies, waits for them, and re-layouts: 27.3 us -> 65.8 us
  matrix products: 119 us -> 103 us
  other arithmetic: 87.1 us -> 75 us
    ppermute x50, waiting for transfers between devices: 261 us -> 136 us  [swap(): return lax.ppermute(piece, AXES, [(i, i ^ 1 << bit) for i in range(count)])]
    concatenate x25 -> x5, other arithmetic: 33.8 us -> 4.13 us  [the longest x1 2.63 us: local(): jnp.concatenate([first_grad, dense_grad], axis=1)]
    unnamed x78 -> x146, local copies, waits for them, and re-layouts: 4.52 us -> 32.1 us
    dot_general x4 -> x5, matrix products: 37.7 us -> 24.1 us  [across(): lax.dot_general(left_side, right_side, (((0,), (0,)), ((), ())), preferre...]
    convert_element_type x17 -> x20, other arithmetic: 18.3 us -> 29.4 us  [the longest x16 24.8 us: take(): self.held = self.held.astype(self.type)]
    select_n x25 -> x44, other arithmetic: 22 us -> 27.3 us  [gather(): held = jnp.where(side == index >> bit & 1, held, got)]
    dot_general x2 -> x3, matrix products: 23.4 us -> 21 us  [the longest x1 12.7 us: local(): jnp.dot(after(activated, *sent), w_down, preferred_element_type=jnp.float32)]
    dot_general x4 -> x5, matrix products: 42 us -> 43.6 us  [against(): lax.dot_general(left_side, right_side, (((1,), (1,)), ((), ())), preferre...]
  transfers between devices with their start and end apart: 50 -> 50, of which waited for: 30 -> 28; matrix products, arithmetic and copies ran while one was open for 18% -> 38% of each run, Pallas kernels for 6% -> 14%
where the time goes in v2:
time: 513 us; the launch traced here: 506 us
  waiting for transfers between devices  136 us (27%)
  matrix products  103 us (20%)
  other arithmetic  75 us (15%)
  Pallas kernels  72.3 us (14%)
  local copies, waits for them, and re-layouts  65.8 us (13%)
  starting transfers between devices  51.6 us (10%)
    ppermute x50, waiting for transfers between devices, swap(): return lax.ppermute(piece, AXES, [(i, i ^ 1 << bit) for i in range(count)])  136 us
    ppermute x50, starting transfers between devices, swap(): return lax.ppermute(piece, AXES, [(i, i ^ 1 << bit) for i in range(count)])  51.6 us
    dot_general x5, matrix products, against(): lax.dot_general(left_side, right_side, (((1,), (1,)), ((), ())), preferre...  43.6 us
    pallas_call x2, Pallas kernels, attend(): pl.pallas_call(functools.partial(attend_kernel, first_head=first_head), g...  36.7 us
    pallas_call x2, Pallas kernels, attend_back(): pl.pallas_call(attend_back_kernel, grid=(buffers, pairs), in_specs=[spec(...  35.6 us
    unnamed x146, local copies, waits for them, and re-layouts  32.1 us
    select_n x44, other arithmetic, gather(): held = jnp.where(side == index >> bit & 1, held, got)  27.3 us
    convert_element_type x16, other arithmetic, take(): self.held = self.held.astype(self.type)  24.8 us
  transfers between devices with their start and end apart: 50, of which 28 were waited for; matrix products, arithmetic and copies ran while one was open for 38% of the time, Pallas kernels for 14%

profile of v2, /device:TPU:0, one launch (start us, length us, event | category | flops | bytes accessed | tf_op | source)
XLA Modules:
  0.0 506.3 jit_solution(2717502591293899925)
XLA Ops:
  0.7 5.5 %concatenate.62 = bf16[384]{0:T(512)(128)(2,1)S(1)} concatenate(bf16[64]{0:T(256)(128)(2,1)} %param.19, bf16[32]{0:T(256)(128)(2,1)} %param.21, bf16[128]{0:T(256)(128)(2,1)} %param.23, bf16[32]{0:T(256)(128)(2,1)} %param.25, bf16[32]{0:T(256)(128)(2,1)} %param.26, bf16[32]{0:T(256)(128)(2,1)} %param.27, bf16[32]{0:T(256)(128)(2,1)} %param.28, bf16[32]{0:T(256)(128)(2,1)} %param.29), dimensions={0} | concatenate | bytes 1536 | tf_op jit(solution)/shard_map/concatenate | solution.py:293
  6.2 4.1 collective-permute-start
  34.7 5.4 %collective-permute-done.6 = bf16[2,1,1,1,1,32,1536]{6,5,0,4,3,2,1:T(8,128)(2,1)S(1)} collective-permute-done((bf16[2,1,1,1,1,32,1536]{6,5,0,4,3,2,1:T(8,128)(2,1)S(1)}, bf16[2,1,1,1,1,32,1536]{6,5,0,4,3,2,1:T(8,128)(2,1)S(1)}, u32[]{:S(2)}, u32[]{:S(2)}) %collective-permute-start.6) | collective-permute-done | bytes 196640 | tf_op jit(solution)/shard_map/ppermute | solution.py:52
  42.1 6.7 %collective-permute-done.11 = bf16[2,1,1,1,1,32,2560]{6,5,0,4,3,2,1:T(8,128)(2,1)S(1)} collective-permute-done((bf16[2,1,1,1,1,32,2560]{6,5,0,4,3,2,1:T(8,128)(2,1)S(1)}, bf16[2,1,1,1,1,32,2560]{6,5,0,4,3,2,1:T(8,128)(2,1)S(1)}, u32[]{:S(2)}, u32[]{:S(2)}) %collective-permute-start.11) | collective-permute-done | bytes 327712 | tf_op jit(solution)/shard_map/ppermute | solution.py:52
  52.4 9.9 %collective-permute-done.15 = bf16[1,1,1,1,1,32,4096]{6,5,4,3,2,1,0:T(8,128)(2,1)S(1)} collective-permute-done((bf16[1,1,1,1,1,32,4096]{6,5,4,3,2,1,0:T(8,128)(2,1)S(1)}, bf16[1,1,1,1,1,32,4096]{6,5,4,3,2,1,0:T(8,128)(2,1)S(1)}, u32[]{:S(2)}, u32[]{:S(2)}) %collective-permute-start.15) | collective-permute-done | bytes 262176 | tf_op jit(solution)/shard_map/ppermute | solution.py:52
  67.3 10.3 %collective-permute-done.16 = bf16[2,1,1,1,1,32,4096]{6,5,0,4,3,2,1:T(8,128)(2,1)S(1)} collective-permute-done((bf16[2,1,1,1,1,32,4096]{6,5,0,4,3,2,1:T(8,128)(2,1)S(1)}, bf16[2,1,1,1,1,32,4096]{6,5,0,4,3,2,1:T(8,128)(2,1)S(1)}, u32[]{:S(2)}, u32[]{:S(2)}) %collective-permute-start.16) | collective-permute-done | bytes 524320 | tf_op jit(solution)/shard_map/ppermute | solution.py:52
  80.4 3.9 collective-permute-done.21
  87.9 16.0 %collective-permute-done.17 = bf16[2,2,1,1,1,32,4096]{6,5,1,0,4,3,2:T(8,128)(2,1)S(1)} collective-permute-done((bf16[2,2,1,1,1,32,4096]{6,5,1,0,4,3,2:T(8,128)(2,1)S(1)}, bf16[2,2,1,1,1,32,4096]{6,5,1,0,4,3,2:T(8,128)(2,1)S(1)}, u32[]{:S(2)}, u32[]{:S(2)}) %collective-permute-start.17) | collective-permute-done | bytes 1048608 | tf_op jit(solution)/shard_map/ppermute | solution.py:52
  106.3 4.9 collective-permute-done.22
  113.0 18.9 %collective-permute-done.13 = bf16[2,2,1,1,2,32,2560]{6,5,4,1,0,3,2:T(8,128)(2,1)S(1)} collective-permute-done((bf16[2,2,1,1,2,32,2560]{6,5,4,1,0,3,2:T(8,128)(2,1)S(1)}, bf16[2,2,1,1,2,32,2560]{6,5,4,1,0,3,2:T(8,128)(2,1)S(1)}, u32[]{:S(2)}, u32[]{:S(2)}) %collective-permute-start.13) | collective-permute-done | bytes 1310752 | tf_op jit(solution)/shard_map/ppermute | solution.py:52
  137.8 13.9 %collective-permute-done.18 = bf16[2,2,2,1,1,32,4096]{6,5,2,1,0,4,3:T(8,128)(2,1)S(1)} collective-permute-done((bf16[2,2,2,1,1,32,4096]{6,5,2,1,0,4,3:T(8,128)(2,1)S(1)}, bf16[2,2,2,1,1,32,4096]{6,5,2,1,0,4,3:T(8,128)(2,1)S(1)}, u32[]{:S(2)}, u32[]{:S(2)}) %collective-permute-start.18) | collective-permute-done | bytes 2097184 | tf_op jit(solution)/shard_map/ppermute | solution.py:52
  154.1 18.4 %shard_map.254 = (bf16[768,512]{1,0:T(8,128)(2,1)S(1)}, bf16[2,8,384,384]{3,2,1,0:T(8,128)(2,1)S(1)}) custom-call(s32[2,3]{1,0:T(2,128)S(1)} %copy-done.10, f32[16]{0:T(128)S(1)} %multiply_exponential_fusion.slopes_ref, bf16[768,1536]{1,0:T(8,128)(2,1)S(1)} %add_convert_fusion.4.q_ref.k_ref.v_ref, bf16[768,1536]{1,0:T(8,128)(2,1)S(1)} %add_convert_fusion.4.q_ref.k_ref.v_ref, ...), custom_call_target="tpu_custom_call" | custom-call | flops 603979776 | bytes 16777216 | tf_op jit(solution)/shard_map/pallas_call | solution.py:162
  181.5 5.4 %add_convert_fusion.3.q_ref.k_ref.v_ref = bf16[768,1536]{1,0:T(8,128)(2,1)S(1)} fusion(bf16[768,1024]{1,0:T(8,128)(2,1)} %copy-done.40, bf16[1024,2560]{1,0:T(8,128)(2,1)S(1)} %bitcast_select_fusion.2, f32[1536]{0:T(1024)S(1)} %get-tuple-element.129), kind=kOutput, calls=%fused_computation.27 | convolution fusion | flops 2418278400 | bytes 7086080 | tf_op jit(solution)/shard_map/dot_general | solution.py:315
  186.9 18.4 %shard_map.255 = (bf16[768,512]{1,0:T(8,128)(2,1)S(1)}, bf16[2,8,384,384]{3,2,1,0:T(8,128)(2,1)S(1)}) custom-call(s32[2,3]{1,0:T(2,128)S(1)} %copy-done.10, f32[16]{0:T(128)S(1)} %multiply_exponential_fusion.slopes_ref, bf16[768,1536]{1,0:T(8,128)(2,1)S(1)} %add_convert_fusion.3.q_ref.k_ref.v_ref, bf16[768,1536]{1,0:T(8,128)(2,1)S(1)} %add_convert_fusion.3.q_ref.k_ref.v_ref, ...), custom_call_target="tpu_custom_call" | custom-call | flops 603979776 | bytes 16777216 | tf_op jit(solution)/shard_map/pallas_call | solution.py:162
  209.6 4.3 bitcast_select_fusion.1
  213.9 12.2 %multiply_convert_fusion = (bf16[768,4096]{1,0:T(8,128)(2,1)S(1)}, f32[768,4096]{1,0:T(8,128)}) fusion(f32[4096]{0:T(1024)S(1)} %slice_bitcast_fusion, bf16[768,1024]{1,0:T(8,128)(2,1)S(1)} %add_convert_fusion.9, bf16[1024,4096]{1,0:T(8,128)(2,1)S(1)} %bitcast_select_fusion.1), kind=kOutput, calls=%fused_computation.8 | convolution fusion | flops 6473908224 | bytes 28852224 | tf_op jit(solution)/shard_map/dot_general | solution.py:327
  226.1 7.5 %convolution_convert_fusion.1 = bf16[4096,1024]{1,0:T(8,128)(2,1)S(1)} fusion(bf16[768,4096]{1,0:T(8,128)(2,1)S(1)} %get-tuple-element.86, bf16[768,1024]{1,0:T(8,128)(2,1)S(1)} %copy-done.34), kind=kOutput, calls=%fused_computation.14 | convolution fusion | flops 6446645248 | bytes 16252928 | tf_op jit(solution)/shard_map/dot_general | solution.py:31
  244.8 20.8 %fusion.45 = (f32[4096]{0:T(1024)}, bf16[768,4096]{1,0:T(8,128)(2,1)}) fusion(f32[768,4096]{1,0:T(8,128)} %get-tuple-element.140, f32[4096]{0:T(1024)S(1)} %slice_bitcast_fusion, bf16[768,1024]{1,0:T(8,128)(2,1)S(1)} %copy-done.35, bf16[4096,1024]{1,0:T(8,128)(2,1)S(1)} %bitcast_select_fusion), kind=kOutput, calls=%fused_computation.204 | convolution fusion | flops 6511652864 | bytes 28868608 | tf_op jit(solution)/shard_map/dot_general | solution.py:37
  265.5 5.8 %add_convert_fusion.1 = bf16[2,2,2,1,2,128,1024]{6,5,4,3,2,1,0:T(8,128)(2,1)S(1)} fusion(bf16[2,2,2,1,2,128,1024]{6,5,4,3,2,1,0:T(8,128)(2,1)} %collective-permute-done.25, bf16[2,2,2,2,2,128,1024]{6,5,4,3,2,1,0:T(8,128)(2,1)} %bitcast.113, s32[]{:T(128)S(6)} %select_n.443), kind=kLoop, calls=%fused_computation.12 | loop fusion | flops 8388608 | bytes 12582916 | tf_op jit(solution)/shard_map/convert_element_type | solution.py:100
  273.9 7.2 %convolution_convert_fusion = bf16[1024,4096]{1,0:T(8,128)(2,1)S(1)} fusion(bf16[768,1024]{1,0:T(8,128)(2,1)S(1)} %copy-done.44, bf16[768,4096]{1,0:T(8,128)(2,1)S(1)} %copy-done.62), kind=kOutput, calls=%fused_computation.13 | convolution fusion | flops 6446645248 | bytes 16252928 | tf_op jit(solution)/shard_map/dot_general | solution.py:31
  288.1 13.5 %multiply_reduce_fusion = (f32[1024]{0:T(1024)S(1)}, f32[768]{0:T(1024)S(1)}, f32[1024]{0:T(1024)S(1)}, f32[768,1024]{1,0:T(8,128)}) fusion(f32[768,1024]{1,0:T(8,128)} %copy-done.14, f32[768]{0:T(1024)S(1)} %fusion.37, f32[768]{0:T(1024)S(1)} %broadcast_multiply_fusion, f32[1024]{0:T(1024)S(1)} %mul.190, bf16[768,4096]{1,0:T(8,128)(2,1)} %get-tuple-element.59, ...), kind=kOutput, calls=%fused_computation.49 | convolution fusion | flops 6448739328 | bytes 20993024 | tf_op jit(solution)/shard_map/dot_general | solution.py:37
  301.8 3.9 fusion.47
  309.1 4.0 add_convert_fusion
  320.5 4.1 copy.29
  324.7 3.9 fusion.27
  332.6 17.8 %shard_map.256 = (bf16[768,512]{1,0:T(8,128)(2,1)S(1)}, bf16[768,512]{1,0:T(8,128)(2,1)S(1)}, bf16[768,512]{1,0:T(8,128)(2,1)S(1)}, f32[2,2,512]{2,1,0:T(2,128)S(1)}) custom-call(bf16[768,512]{1,0:T(8,128)(2,1)S(1)} %get-tuple-element.107.g_ref, bf16[2,8,384,384]{3,2,1,0:T(8,128)(2,1)S(1)} %copy-done.5, bf16[768,1536]{1,0:T(8,128)(2,1)S(1)} %copy-done.1, ...), custom_call_target="tpu_custom_call" | custom-call | flops 1509949440 | bytes 20971520 | tf_op jit(solution)/shard_map/pallas_call | solution.py:224
  371.9 17.8 %shard_map.257 = (bf16[768,512]{1,0:T(8,128)(2,1)S(1)}, bf16[768,512]{1,0:T(8,128)(2,1)S(1)}, bf16[768,512]{1,0:T(8,128)(2,1)S(1)}, f32[2,2,512]{2,1,0:T(2,128)S(1)}) custom-call(bf16[768,512]{1,0:T(8,128)(2,1)S(1)} %get-tuple-element.70.g_ref, bf16[2,8,384,384]{3,2,1,0:T(8,128)(2,1)S(1)} %copy-done.3, ...), custom_call_target="tpu_custom_call" | custom-call | flops 1509949440 | bytes 20971520 | tf_op jit(solution)/shard_map/pallas_call | solution.py:224
  434.8 6.1 %collective-permute-done.49 = bf16[1,1,1,1,1,128,1024]{6,5,4,3,2,1,0:T(8,128)(2,1)} collective-permute-done((bf16[1,1,1,1,1,128,1024]{6,5,4,3,2,1,0:T(8,128)(2,1)S(1)}, bf16[1,1,1,1,1,128,1024]{6,5,4,3,2,1,0:T(8,128)(2,1)}, u32[]{:S(2)}, u32[]{:S(2)}) %collective-permute-start.49) | collective-permute-done | bytes 262176 | tf_op jit(solution)/shard_map/ppermute | solution.py:52
  450.9 12.7 %add_convert_fusion.7 = bf16[768,1024]{1,0:T(8,128)(2,1)} fusion(f32[768,1024]{1,0:T(8,128)} %copy-done.14, bf16[768,4096]{1,0:T(8,128)(2,1)} %copy-done.63, bf16[4096,1024]{1,0:T(8,128)(2,1)} %copy-done.25, f32[1024]{0:T(1024)S(1)} %add.324), kind=kOutput, calls=%fused_computation.47 | convolution fusion | flops 6444810240 | bytes 19402752 | tf_op jit(solution)/shard_map/dot_general | solution.py:406
  486.4 4.2 collective-permute-done.40
  490.8 4.8 collective-permute-done.37
  496.0 5.6 %collective-permute-done.41 = bf16[1,1,1,1,1,32,1536]{6,5,4,3,2,1,0:T(8,128)(2,1)S(1)} collective-permute-done((bf16[1,1,1,1,1,32,1536]{6,5,4,3,2,1,0:T(8,128)(2,1)S(1)}, bf16[1,1,1,1,1,32,1536]{6,5,4,3,2,1,0:T(8,128)(2,1)S(1)}, u32[]{:S(2)}, u32[]{:S(2)}) %collective-permute-start.41) | collective-permute-done | bytes 98336 | tf_op jit(solution)/shard_map/ppermute | solution.py:52
  (410 shorter events, 205.9 us)
Async XLA Ops:
  11.2 20.9 %collective-permute-start.5 = (bf16[1,1,1,1,1,32,1536]{6,5,4,3,2,1,0:T(8,128)(2,1)S(1)}, bf16[1,1,1,1,1,32,1536]{6,5,4,3,2,1,0:T(8,128)(2,1)S(1)}, u32[]{:S(2)}, u32[]{:S(2)}) collective-permute-start(bf16[1,1,1,1,1,32,1536]{6,5,4,3,2,1,0:T(8,128)(2,1)S(1)} %get-tuple-element.118), channel_id=1, source_target_pairs={{0,16},{1,17},{2,18},{3,19},{4,20},{5,21},{6,22},{7,23},{8,24},{9,... | collective-permute-start | bytes 294920 | tf_op jit(solution)/shard_map/ppermute | solution.py:52
  12.1 21.7 %collective-permute-start.10 = (bf16[1,1,1,1,1,32,2560]{6,5,4,3,2,1,0:T(8,128)(2,1)S(1)}, bf16[1,1,1,1,1,32,2560]{6,5,4,3,2,1,0:T(8,128)(2,1)S(1)}, u32[]{:S(2)}, u32[]{:S(2)}) collective-permute-start(bf16[1,1,1,1,1,32,2560]{6,5,4,3,2,1,0:T(8,128)(2,1)S(1)} %get-tuple-element.116), channel_id=1, source_target_pairs={{0,16},{1,17},{2,18},{3,19},{4,20},{5,21},{6,22},{7,23},{8,24},{9,... | collective-permute-start | bytes 491528 | tf_op jit(solution)/shard_map/ppermute | solution.py:52
  34.0 14.8 %collective-permute-start.11 = (bf16[2,1,1,1,1,32,2560]{6,5,0,4,3,2,1:T(8,128)(2,1)S(1)}, bf16[2,1,1,1,1,32,2560]{6,5,0,4,3,2,1:T(8,128)(2,1)S(1)}, u32[]{:S(2)}, u32[]{:S(2)}) collective-permute-start(bf16[2,1,1,1,1,32,2560]{6,5,0,4,3,2,1:T(8,128)(2,1)S(1)} %broadcast_select_fusion.28), channel_id=1, source_target_pairs={{0,8},{1,9},{2,10},{3,11},{4,12},{5,13},{6,14},{7,15},{8,0},{9,1},... | collective-permute-start | bytes 983048 | tf_op jit(solution)/shard_map/ppermute | solution.py:52
  40.3 22.3 %collective-permute-start.7 = (bf16[2,2,1,1,1,32,1536]{6,5,1,0,4,3,2:T(8,128)(2,1)S(1)}, bf16[2,2,1,1,1,32,1536]{6,5,1,0,4,3,2:T(8,128)(2,1)S(1)}, u32[]{:S(2)}, u32[]{:S(2)}) collective-permute-start(bf16[2,2,1,1,1,32,1536]{6,5,1,0,4,3,2:T(8,128)(2,1)S(1)} %broadcast_select_fusion.26), channel_id=1, source_target_pairs={{0,4},{1,5},{2,6},{3,7},{4,0},{5,1},{6,2},{7,3},{8,12},{9,13},{10,... | collective-permute-start | bytes 1179656 | tf_op jit(solution)/shard_map/ppermute | solution.py:52
  41.8 20.4 %collective-permute-start.15 = (bf16[1,1,1,1,1,32,4096]{6,5,4,3,2,1,0:T(8,128)(2,1)S(1)}, bf16[1,1,1,1,1,32,4096]{6,5,4,3,2,1,0:T(8,128)(2,1)S(1)}, u32[]{:S(2)}, u32[]{:S(2)}) collective-permute-start(bf16[1,1,1,1,1,32,4096]{6,5,4,3,2,1,0:T(8,128)(2,1)S(1)} %bitcast.141), channel_id=1, source_target_pairs={{0,16},{1,17},{2,18},{3,19},{4,20},{5,21},{6,22},{7,23},{8,24},{9,... | collective-permute-start | bytes 786440 | tf_op jit(solution)/shard_map/ppermute | solution.py:52
  49.1 28.8 %collective-permute-start.12 = (bf16[2,2,1,1,1,32,2560]{6,5,1,0,4,3,2:T(8,128)(2,1)S(1)}, bf16[2,2,1,1,1,32,2560]{6,5,1,0,4,3,2:T(8,128)(2,1)S(1)}, u32[]{:S(2)}, u32[]{:S(2)}) collective-permute-start(bf16[2,2,1,1,1,32,2560]{6,5,1,0,4,3,2:T(8,128)(2,1)S(1)} %broadcast_select_fusion.20), channel_id=1, source_target_pairs={{0,1},{1,0},{2,3},{3,2},{4,5},{5,4},{6,7},{7,6},{8,9},{9,8},{10,11... | collective-permute-start | bytes 1966088 | tf_op jit(solution)/shard_map/ppermute | solution.py:52
  50.7 15.6 %collective-permute-start.20 = (bf16[1,1,1,1,1,128,1024]{6,5,4,3,2,1,0:T(8,128)(2,1)S(1)}, bf16[1,1,1,1,1,128,1024]{6,5,4,3,2,1,0:T(8,128)(2,1)S(1)}, u32[]{:S(2)}, u32[]{:S(2)}) collective-permute-start(bf16[1,1,1,1,1,128,1024]{6,5,4,3,2,1,0:T(8,128)(2,1)S(1)} %bitcast.142), channel_id=1, source_target_pairs={{0,16},{1,17},{2,18},{3,19},{4,20},{5,21},{6,22},{7,23},{8,24},{9,... | collective-permute-start | bytes 786440 | tf_op jit(solution)/shard_map/ppermute | solution.py:52
  62.5 15.1 %collective-permute-start.16 = (bf16[2,1,1,1,1,32,4096]{6,5,0,4,3,2,1:T(8,128)(2,1)S(1)}, bf16[2,1,1,1,1,32,4096]{6,5,0,4,3,2,1:T(8,128)(2,1)S(1)}, u32[]{:S(2)}, u32[]{:S(2)}) collective-permute-start(bf16[2,1,1,1,1,32,4096]{6,5,0,4,3,2,1:T(8,128)(2,1)S(1)} %broadcast_select_fusion.24), channel_id=1, source_target_pairs={{0,8},{1,9},{2,10},{3,11},{4,12},{5,13},{6,14},{7,15},{8,0},{9,1},... | collective-permute-start | bytes 1572872 | tf_op jit(solution)/shard_map/ppermute | solution.py:52
  62.8 24.5 %collective-permute-start.8 = (bf16[2,2,2,1,1,32,1536]{6,5,2,1,0,4,3:T(8,128)(2,1)S(1)}, bf16[2,2,2,1,1,32,1536]{6,5,2,1,0,4,3:T(8,128)(2,1)S(1)}, u32[]{:S(2)}, u32[]{:S(2)}) collective-permute-start(bf16[2,2,2,1,1,32,1536]{6,5,2,1,0,4,3:T(8,128)(2,1)S(1)} %broadcast_select_fusion.18), channel_id=1, source_target_pairs={{0,1},{1,0},{2,3},{3,2},{4,5},{5,4},{6,7},{7,6},{8,9},{9,8},{10,11... | collective-permute-start | bytes 2359304 | tf_op jit(solution)/shard_map/ppermute | solution.py:52
  66.4 17.9 %collective-permute-start.21 = (bf16[2,1,1,1,1,128,1024]{6,5,0,4,3,2,1:T(8,128)(2,1)S(1)}, bf16[2,1,1,1,1,128,1024]{6,5,0,4,3,2,1:T(8,128)(2,1)S(1)}, u32[]{:S(2)}, u32[]{:S(2)}) collective-permute-start(bf16[2,1,1,1,1,128,1024]{6,5,0,4,3,2,1:T(8,128)(2,1)S(1)} %broadcast_select_fusion.22), channel_id=1, source_target_pairs={{0,8},{1,9},{2,10},{3,11},{4,12},{5,13},{6,14},{7,15},{8,0},{9,1},... | collective-permute-start | bytes 1572872 | tf_op jit(solution)/shard_map/ppermute | solution.py:52
  77.7 26.2 %collective-permute-start.17 = (bf16[2,2,1,1,1,32,4096]{6,5,1,0,4,3,2:T(8,128)(2,1)S(1)}, bf16[2,2,1,1,1,32,4096]{6,5,1,0,4,3,2:T(8,128)(2,1)S(1)}, u32[]{:S(2)}, u32[]{:S(2)}) collective-permute-start(bf16[2,2,1,1,1,32,4096]{6,5,1,0,4,3,2:T(8,128)(2,1)S(1)} %broadcast_select_fusion.16), channel_id=1, source_target_pairs={{0,4},{1,5},{2,6},{3,7},{4,0},{5,1},{6,2},{7,3},{8,12},{9,13},{10,... | collective-permute-start | bytes 3145736 | tf_op jit(solution)/shard_map/ppermute | solution.py:52
  78.3 53.6 %collective-permute-start.13 = (bf16[2,2,1,1,2,32,2560]{6,5,4,1,0,3,2:T(8,128)(2,1)S(1)}, bf16[2,2,1,1,2,32,2560]{6,5,4,1,0,3,2:T(8,128)(2,1)S(1)}, u32[]{:S(2)}, u32[]{:S(2)}) collective-permute-start(bf16[2,2,1,1,2,32,2560]{6,5,4,1,0,3,2:T(8,128)(2,1)S(1)} %broadcast_select_fusion.12), channel_id=1, source_target_pairs={{0,4},{1,5},{2,6},{3,7},{4,0},{5,1},{6,2},{7,3},{8,12},{9,13},{10,... | collective-permute-start | bytes 3932168 | tf_op jit(solution)/shard_map/ppermute | solution.py:52
  84.5 26.7 %collective-permute-start.22 = (bf16[2,2,1,1,1,128,1024]{6,5,1,0,4,3,2:T(8,128)(2,1)S(1)}, bf16[2,2,1,1,1,128,1024]{6,5,1,0,4,3,2:T(8,128)(2,1)S(1)}, u32[]{:S(2)}, u32[]{:S(2)}) collective-permute-start(bf16[2,2,1,1,1,128,1024]{6,5,1,0,4,3,2:T(8,128)(2,1)S(1)} %broadcast_select_fusion.14), channel_id=1, source_target_pairs={{0,1},{1,0},{2,3},{3,2},{4,5},{5,4},{6,7},{7,6},{8,9},{9,8},{10,11... | collective-permute-start | bytes 3145736 | tf_op jit(solution)/shard_map/ppermute | solution.py:52
  87.6 46.4 %collective-permute-start.9 = (bf16[2,2,2,1,2,32,1536]{6,5,4,2,1,0,3:T(8,128)(2,1)S(1)}, bf16[2,2,2,1,2,32,1536]{6,5,4,2,1,0,3:T(8,128)(2,1)S(1)}, u32[]{:S(2)}, u32[]{:S(2)}) collective-permute-start(bf16[2,2,2,1,2,32,1536]{6,5,4,2,1,0,3:T(8,128)(2,1)S(1)} %broadcast_select_fusion.10), channel_id=1, source_target_pairs={{0,2},{1,3},{2,0},{3,1},{4,6},{5,7},{6,4},{7,5},{8,10},{9,11},{10,... | collective-permute-start | bytes 4718600 | tf_op jit(solution)/shard_map/ppermute | solution.py:52
  104.1 47.6 %collective-permute-start.18 = (bf16[2,2,2,1,1,32,4096]{6,5,2,1,0,4,3:T(8,128)(2,1)S(1)}, bf16[2,2,2,1,1,32,4096]{6,5,2,1,0,4,3:T(8,128)(2,1)S(1)}, u32[]{:S(2)}, u32[]{:S(2)}) collective-permute-start(bf16[2,2,2,1,1,32,4096]{6,5,2,1,0,4,3:T(8,128)(2,1)S(1)} %broadcast_select_fusion.8), channel_id=1, source_target_pairs={{0,1},{1,0},{2,3},{3,2},{4,5},{5,4},{6,7},{7,6},{8,9},{9,8},{10,11... | collective-permute-start | bytes 6291464 | tf_op jit(solution)/shard_map/ppermute | solution.py:52
  112.8 63.2 %collective-permute-start.23 = (bf16[2,2,1,1,2,128,1024]{6,5,4,1,0,3,2:T(8,128)(2,1)}, bf16[2,2,1,1,2,128,1024]{6,5,4,1,0,3,2:T(8,128)(2,1)S(1)}, u32[]{:S(2)}, u32[]{:S(2)}) collective-permute-start(bf16[2,2,1,1,2,128,1024]{6,5,4,1,0,3,2:T(8,128)(2,1)} %broadcast_select_fusion.6), channel_id=1, source_target_pairs={{0,4},{1,5},{2,6},{3,7},{4,0},{5,1},{6,2},{7,3},{8,12},{9,13},{10,... | collective-permute-start | bytes 6291464 | tf_op jit(solution)/shard_map/ppermute | solution.py:52
  133.7 45.3 %collective-permute-start.14 = (bf16[2,2,2,1,2,32,2560]{6,5,4,2,1,0,3:T(8,128)(2,1)}, bf16[2,2,2,1,2,32,2560]{6,5,4,2,1,0,3:T(8,128)(2,1)}, u32[]{:S(2)}, u32[]{:S(2)}) collective-permute-start(bf16[2,2,2,1,2,32,2560]{6,5,4,2,1,0,3:T(8,128)(2,1)} %broadcast_select_fusion.4), channel_id=1, source_target_pairs={{0,2},{1,3},{2,0},{3,1},{4,6},{5,7},{6,4},{7,5},{8,10},{9,11},{10,... | collective-permute-start | bytes 7864328 | tf_op jit(solution)/shard_map/ppermute | solution.py:52
  154.1 55.5 %collective-permute-start.19 = (bf16[2,2,2,1,2,32,4096]{6,5,4,2,1,0,3:T(8,128)(2,1)}, bf16[2,2,2,1,2,32,4096]{6,5,4,2,1,0,3:T(8,128)(2,1)}, u32[]{:S(2)}, u32[]{:S(2)}) collective-permute-start(bf16[2,2,2,1,2,32,4096]{6,5,4,2,1,0,3:T(8,128)(2,1)} %broadcast_select_fusion.2), channel_id=1, source_target_pairs={{0,2},{1,3},{2,0},{3,1},{4,6},{5,7},{6,4},{7,5},{8,10},{9,11},{10,... | collective-permute-start | bytes 12582920 | tf_op jit(solution)/shard_map/ppermute | solution.py:52
  178.6 62.5 %collective-permute-start.24 = (bf16[2,2,2,1,2,128,1024]{6,5,4,2,1,0,3:T(8,128)(2,1)}, bf16[2,2,2,1,2,128,1024]{6,5,4,2,1,0,3:T(8,128)(2,1)}, u32[]{:S(2)}, u32[]{:S(2)}) collective-permute-start(bf16[2,2,2,1,2,128,1024]{6,5,4,2,1,0,3:T(8,128)(2,1)} %broadcast_select_fusion), channel_id=1, source_target_pairs={{0,2},{1,3},{2,0},{3,1},{4,6},{5,7},{6,4},{7,5},{8,10},{9,11},{10,... | collective-permute-start | bytes 12582920 | tf_op jit(solution)/shard_map/ppermute | solution.py:52
  238.3 27.2 %collective-permute-start.25 = (bf16[2,2,2,1,2,128,1024]{6,5,4,3,2,1,0:T(8,128)(2,1)}, bf16[2,2,2,1,2,128,1024]{6,5,4,3,2,1,0:T(8,128)(2,1)}, u32[]{:S(2)}, u32[]{:S(2)}) collective-permute-start(bf16[2,2,2,1,2,128,1024]{6,5,4,3,2,1,0:T(8,128)(2,1)} %constant_dynamic-slice_fusion.28), channel_id=1, source_target_pairs={{0,2},{1,3},{2,0},{3,1},{4,6},{5,7},{6,4},{7,5},{8,10},{9,11},{10,... | collective-permute-start | bytes 12582920 | tf_op jit(solution)/shard_map/ppermute | solution.py:52
  285.9 23.2 %collective-permute-start.26 = (bf16[2,2,2,1,2,32,4096]{6,5,4,3,2,1,0:T(8,128)(2,1)}, bf16[2,2,2,1,2,32,4096]{6,5,4,3,2,1,0:T(8,128)(2,1)}, u32[]{:S(2)}, u32[]{:S(2)}) collective-permute-start(bf16[2,2,2,1,2,32,4096]{6,5,4,3,2,1,0:T(8,128)(2,1)} %constant_dynamic-slice_fusion.26), channel_id=1, source_target_pairs={{0,2},{1,3},{2,0},{3,1},{4,6},{5,7},{6,4},{7,5},{8,10},{9,11},{10,... | collective-permute-start | bytes 12582920 | tf_op jit(solution)/shard_map/ppermute | solution.py:52
  286.4 64.2 %collective-permute-start.27 = (bf16[2,2,2,1,1,128,1024]{6,5,4,3,2,1,0:T(8,128)(2,1)}, bf16[2,2,2,1,1,128,1024]{6,5,4,3,2,1,0:T(8,128)(2,1)}, u32[]{:S(2)}, u32[]{:S(2)}) collective-permute-start(bf16[2,2,2,1,1,128,1024]{6,5,4,3,2,1,0:T(8,128)(2,1)} %constant_dynamic-slice_fusion.27), channel_id=1, source_target_pairs={{0,1},{1,0},{2,3},{3,2},{4,5},{5,4},{6,7},{7,6},{8,9},{9,8},{10,11... | collective-permute-start | bytes 6291464 | tf_op jit(solution)/shard_map/ppermute | solution.py:52
  324.7 72.5 %collective-permute-start.28 = (bf16[2,2,1,1,2,32,4096]{6,5,4,3,2,1,0:T(8,128)(2,1)}, bf16[2,2,1,1,2,32,4096]{6,5,4,3,2,1,0:T(8,128)(2,1)}, u32[]{:S(2)}, u32[]{:S(2)}) collective-permute-start(bf16[2,2,1,1,2,32,4096]{6,5,4,3,2,1,0:T(8,128)(2,1)} %constant_dynamic-slice_fusion.25), channel_id=1, source_target_pairs={{0,4},{1,5},{2,6},{3,7},{4,0},{5,1},{6,2},{7,3},{8,12},{9,13},{10,... | collective-permute-start | bytes 6291464 | tf_op jit(solution)/shard_map/ppermute | solution.py:52
  358.4 36.5 %collective-permute-start.29 = (bf16[2,2,1,1,1,128,1024]{6,5,4,3,2,1,0:T(8,128)(2,1)}, bf16[2,2,1,1,1,128,1024]{6,5,4,3,2,1,0:T(8,128)(2,1)}, u32[]{:S(2)}, u32[]{:S(2)}) collective-permute-start(bf16[2,2,1,1,1,128,1024]{6,5,4,3,2,1,0:T(8,128)(2,1)} %constant_dynamic-slice_fusion.24), channel_id=1, source_target_pairs={{0,4},{1,5},{2,6},{3,7},{4,0},{5,1},{6,2},{7,3},{8,12},{9,13},{10,... | collective-permute-start | bytes 3145736 | tf_op jit(solution)/shard_map/ppermute | solution.py:52
  369.5 38.6 %collective-permute-start.31 = (bf16[2,2,2,1,2,32,2560]{6,5,4,3,2,1,0:T(8,128)(2,1)}, bf16[2,2,2,1,2,32,2560]{6,5,4,3,2,1,0:T(8,128)(2,1)}, u32[]{:S(2)}, u32[]{:S(2)}) collective-permute-start(bf16[2,2,2,1,2,32,2560]{6,5,4,3,2,1,0:T(8,128)(2,1)} %constant_dynamic-slice_fusion.23), channel_id=1, source_target_pairs={{0,2},{1,3},{2,0},{3,1},{4,6},{5,7},{6,4},{7,5},{8,10},{9,11},{10,... | collective-permute-start | bytes 7864328 | tf_op jit(solution)/shard_map/ppermute | solution.py:52
  397.0 25.8 %collective-permute-start.34 = (bf16[2,1,1,1,1,128,1024]{6,5,4,3,2,1,0:T(8,128)(2,1)S(1)}, bf16[2,1,1,1,1,128,1024]{6,5,4,3,2,1,0:T(8,128)(2,1)S(1)}, u32[]{:S(2)}, u32[]{:S(2)}) collective-permute-start(bf16[2,1,1,1,1,128,1024]{6,5,4,3,2,1,0:T(8,128)(2,1)S(1)} %constant_dynamic-slice_fusion.21), channel_id=1, source_target_pairs={{0,8},{1,9},{2,10},{3,11},{4,12},{5,13},{6,14},{7,15},{8,0},{9,1},... | collective-permute-start | bytes 1572872 | tf_op jit(solution)/shard_map/ppermute | solution.py:52
  400.1 25.6 %collective-permute-start.33 = (bf16[2,2,1,1,1,32,4096]{6,5,4,3,2,1,0:T(8,128)(2,1)S(1)}, bf16[2,2,1,1,1,32,4096]{6,5,4,3,2,1,0:T(8,128)(2,1)S(1)}, u32[]{:S(2)}, u32[]{:S(2)}) collective-permute-start(bf16[2,2,1,1,1,32,4096]{6,5,4,3,2,1,0:T(8,128)(2,1)S(1)} %constant_dynamic-slice_fusion.22), channel_id=1, source_target_pairs={{0,1},{1,0},{2,3},{3,2},{4,5},{5,4},{6,7},{7,6},{8,9},{9,8},{10,11... | collective-permute-start | bytes 3145736 | tf_op jit(solution)/shard_map/ppermute | solution.py:52
  426.2 14.7 %collective-permute-start.49 = (bf16[1,1,1,1,1,128,1024]{6,5,4,3,2,1,0:T(8,128)(2,1)S(1)}, bf16[1,1,1,1,1,128,1024]{6,5,4,3,2,1,0:T(8,128)(2,1)}, u32[]{:S(2)}, u32[]{:S(2)}) collective-permute-start(bf16[1,1,1,1,1,128,1024]{6,5,4,3,2,1,0:T(8,128)(2,1)S(1)} %constant_dynamic-slice_fusion.14), channel_id=1, source_target_pairs={{0,16},{1,17},{2,18},{3,19},{4,20},{5,21},{6,22},{7,23},{8,24},{9,... | collective-permute-start | bytes 786440 | tf_op jit(solution)/shard_map/ppermute | solution.py:52
  428.4 18.2 %collective-permute-start.47 = (bf16[2,1,1,1,1,32,4096]{6,5,4,3,2,1,0:T(8,128)(2,1)}, bf16[2,1,1,1,1,32,4096]{6,5,4,3,2,1,0:T(8,128)(2,1)}, u32[]{:S(2)}, u32[]{:S(2)}) collective-permute-start(bf16[2,1,1,1,1,32,4096]{6,5,4,3,2,1,0:T(8,128)(2,1)} %constant_dynamic-slice_fusion.15), channel_id=1, source_target_pairs={{0,8},{1,9},{2,10},{3,11},{4,12},{5,13},{6,14},{7,15},{8,0},{9,1},... | collective-permute-start | bytes 1572872 | tf_op jit(solution)/shard_map/ppermute | solution.py:52
  430.1 37.0 %collective-permute-start.35 = (bf16[2,2,2,1,1,32,2560]{6,5,4,3,2,1,0:T(8,128)(2,1)}, bf16[2,2,2,1,1,32,2560]{6,5,4,3,2,1,0:T(8,128)(2,1)}, u32[]{:S(2)}, u32[]{:S(2)}) collective-permute-start(bf16[2,2,2,1,1,32,2560]{6,5,4,3,2,1,0:T(8,128)(2,1)} %constant_dynamic-slice_fusion.18), channel_id=1, source_target_pairs={{0,1},{1,0},{2,3},{3,2},{4,5},{5,4},{6,7},{7,6},{8,9},{9,8},{10,11... | collective-permute-start | bytes 3932168 | tf_op jit(solution)/shard_map/ppermute | solution.py:52
  430.7 18.8 %collective-permute-start.32 = (bf16[2,2,1,1,2,32,1536]{6,5,4,3,2,1,0:T(8,128)(2,1)}, bf16[2,2,1,1,2,32,1536]{6,5,4,3,2,1,0:T(8,128)(2,1)}, u32[]{:S(2)}, u32[]{:S(2)}) collective-permute-start(bf16[2,2,1,1,2,32,1536]{6,5,4,3,2,1,0:T(8,128)(2,1)} %constant_dynamic-slice_fusion.19), channel_id=1, source_target_pairs={{0,4},{1,5},{2,6},{3,7},{4,0},{5,1},{6,2},{7,3},{8,12},{9,13},{10,... | collective-permute-start | bytes 2359304 | tf_op jit(solution)/shard_map/ppermute | solution.py:52
  434.7 28.8 %collective-permute-start.42 = (f32[2,2,2,1,2,1,384]{6,5,4,3,2,1,0:T(1,128)S(1)}, f32[2,2,2,1,2,1,384]{6,5,4,3,2,1,0:T(1,128)S(1)}, u32[]{:S(2)}, u32[]{:S(2)}) collective-permute-start(f32[2,2,2,1,2,1,384]{6,5,4,3,2,1,0:T(1,128)S(1)} %constant_dynamic-slice_fusion.17), channel_id=1, source_target_pairs={{0,2},{1,3},{2,0},{3,1},{4,6},{5,7},{6,4},{7,5},{8,10},{9,11},{10,... | collective-permute-start | bytes 73736 | tf_op jit(solution)/shard_map/ppermute | solution.py:52
  (86 other events, 732.1 us)
